TPU v7x, 128 devices: a whole 4x4x4 slice. The times are simulated.
128 devices in a mesh: gx: 8 (over z, core), yz: 16 (over y, x).
Axes of the slice: x: 4, y: 4, z: 4, core: 2. Of those that a mesh axis runs over, the one named last changes fastest.
Arguments:
- tokens: bfloat16 [2, 256, 10240], P(None, 'gx', 'yz'), may hold values from -16 to 16
- norm_gain: float32 [10240], P('yz'), may hold values from 0.5 to 1.5
- w_query: bfloat16 [10240, 12288], P('yz', 'gx'), may hold values from -0.0625 to 0.0625
- w_shared: bfloat16 [10240, 512], P('yz'), may hold values from -0.0625 to 0.0625
- w_gate: bfloat16 [10240, 36864], P('yz', 'gx'), may hold values from -0.0625 to 0.0625
- w_up: bfloat16 [10240, 36864], P('yz', 'gx'), may hold values from -0.0625 to 0.0625
- w_out: bfloat16 [12288, 10240], P('gx', 'yz'), may hold values from -0.0546875 to 0.0546875
- w_down: bfloat16 [36864, 10240], P('gx', 'yz'), may hold values from -0.03125 to 0.03125
- key_cache: bfloat16 [256, 2048, 256], P(('gx', 'yz')), may hold values from -512 to 512
- value_cache: bfloat16 [256, 2048, 256], P(('gx', 'yz')), may hold values from -12 to 12
- lengths: int32 [256], P(('gx', 'yz')), may hold values from 1 to 2048, as said below
Outputs:
- layer_out: bfloat16 [2, 256, 10240], P(None, 'gx', 'yz')
- new_entries: bfloat16 [2, 256, 512], P(None, ('gx', 'yz'))
Inputs may be any that keep to these rules, and one draw needn't show every extreme that they name: Row r's caches hold live entries in their first lengths[r] slots; at least one row's cache is full.
All inputs are finite; a program needn't handle non-finite values.
Results may differ from a plain program's by a relative error of at most 0.0084.
Values may be sent and summed in bfloat16 or wider, within the bound.
A program may use at most 192 MiB of HBM per device.

v0:
```python
import math

import jax
import jax.numpy as jnp
from jax import lax
from jax.sharding import PartitionSpec as P

EPSILON = 1e-06


def rotate_pairs(vectors, positions):
    half_dim = vectors.shape[-1] // 2
    frequency = jnp.exp(
        jnp.arange(half_dim, dtype=jnp.float32) * (-2.0 * math.log(10000.0) / vectors.shape[-1])
    )
    angles = positions[:, None, None] * frequency
    cosine = jnp.cos(angles)
    sine_part = jnp.sin(angles)
    front_part = vectors[..., :half_dim]
    back_part = vectors[..., half_dim:]
    return jnp.concatenate(
        [front_part * cosine - back_part * sine_part, back_part * cosine + front_part * sine_part],
        axis=-1,
    )


def attend(query_heads, key_cache, value_cache, lengths, new_keys, new_values):
    head_dim = query_heads.shape[-1]
    factor = 1.0 / math.sqrt(head_dim)
    cached = (
        jnp.einsum("rhd,rcd->rhc", query_heads, key_cache, preferred_element_type=jnp.float32)
        * factor
    )
    slot_index = jnp.arange(key_cache.shape[1], dtype=jnp.int32)
    live_mask = slot_index[None, None, :] < lengths[:, None, None]
    cached = jnp.where(live_mask, cached, -jnp.inf)
    fresh_scores = (
        jnp.einsum("rhd,rnd->rhn", query_heads, new_keys, preferred_element_type=jnp.float32)
        * factor
    )
    row_top = jnp.maximum(jnp.max(cached, axis=2), jnp.max(fresh_scores, axis=2))[:, :, None]
    cached_exp = jnp.exp(cached - row_top)
    fresh_exp = jnp.exp(fresh_scores - row_top)
    denominator = jnp.sum(cached_exp, axis=2, keepdims=True) + jnp.sum(
        fresh_exp, axis=2, keepdims=True
    )
    cached_weight = (cached_exp / denominator).astype(jnp.bfloat16)
    fresh_weight = (fresh_exp / denominator).astype(jnp.bfloat16)
    attended = jnp.einsum(
        "rhc,rcd->rhd", cached_weight, value_cache, preferred_element_type=jnp.float32
    )
    attended = attended + jnp.einsum(
        "rhn,rnd->rhd", fresh_weight, new_values, preferred_element_type=jnp.float32
    )
    return attended.astype(jnp.bfloat16)


def local(
    tokens,
    norm_gain,
    w_query,
    w_shared,
    w_gate,
    w_up,
    w_out,
    w_down,
    key_cache,
    value_cache,
    lengths,
):
    groups = lax.axis_size("gx")
    lane_count = lax.axis_size("yz")
    group_index = lax.axis_index("gx")
    step_count = tokens.shape[0]
    block_rows = tokens.shape[1]
    columns = tokens.shape[2]
    local_rows = key_cache.shape[0]
    head_dim = key_cache.shape[2]
    query_cols = w_query.shape[1]
    hidden_cols = w_gate.shape[1]
    total_rows = block_rows * groups
    model_width = columns * lane_count
    heads_all = query_cols * groups // head_dim
    shared_start = query_cols + 2 * hidden_cols
    fresh_keys = []
    fresh_values = []
    outputs = []
    entries = []
    for step_index in range(step_count):
        current = tokens[step_index]
        current_float = current.astype(jnp.float32)
        squares = jnp.sum(current_float * current_float, axis=1)
        square_total = lax.psum(squares, "yz")
        inverse_rms = lax.rsqrt(square_total / model_width + EPSILON)
        normed = (current_float * inverse_rms[:, None] * norm_gain).astype(jnp.bfloat16)
        shaped = normed.reshape(lane_count, local_rows, columns)
        gathered = lax.all_gather(shaped, "gx", axis=1, tiled=True).reshape(total_rows, columns)
        summed = lax.psum_scatter(
            jnp.concatenate(
                [
                    jnp.dot(gathered, w_query, preferred_element_type=jnp.float32),
                    jnp.dot(gathered, w_gate, preferred_element_type=jnp.float32),
                    jnp.dot(gathered, w_up, preferred_element_type=jnp.float32),
                    jnp.dot(gathered, w_shared, preferred_element_type=jnp.float32),
                ],
                axis=1,
            ),
            "yz",
            scatter_dimension=0,
            tiled=True,
        )
        query_part = summed[:, :query_cols]
        shared_rows = lax.dynamic_slice_in_dim(
            summed[:, shared_start:], group_index * local_rows, local_rows, 0
        )
        hidden = (
            jax.nn.silu(summed[:, query_cols : query_cols + hidden_cols])
            * summed[:, query_cols + hidden_cols : shared_start]
        ).astype(jnp.bfloat16)
        query_block = query_part.astype(jnp.bfloat16)
        query_local = lax.all_to_all(query_block, "gx", split_axis=0, concat_axis=1, tiled=True)
        positions = (lengths + step_index).astype(jnp.float32)
        query_heads = rotate_pairs(
            query_local.astype(jnp.float32).reshape(local_rows, heads_all, head_dim), positions
        ).astype(jnp.bfloat16)
        key_round = lax.optimization_barrier(shared_rows[:, :head_dim].astype(jnp.bfloat16)).astype(
            jnp.float32
        )
        key_now = rotate_pairs(key_round[:, None, :], positions)[:, 0, :].astype(jnp.bfloat16)
        value_now = shared_rows[:, head_dim:].astype(jnp.bfloat16)
        fresh_keys.append(key_now)
        fresh_values.append(value_now)
        new_keys = jnp.stack(fresh_keys, axis=1)
        new_values = jnp.stack(fresh_values, axis=1)
        attended = attend(
            query_heads, key_cache, value_cache, lengths, new_keys, new_values
        ).reshape(local_rows, heads_all * head_dim)
        returned = lax.all_to_all(attended, "gx", split_axis=1, concat_axis=0, tiled=True)
        joined = jnp.concatenate([returned, hidden], axis=1)
        piece_rows = lax.all_gather(joined, "yz", axis=0, tiled=True)
        partial_value = jnp.dot(
            piece_rows[:, :query_cols], w_out, preferred_element_type=jnp.float32
        ) + jnp.dot(piece_rows[:, query_cols:], w_down, preferred_element_type=jnp.float32)
        shaped_sum = partial_value.reshape(lane_count, groups, local_rows, columns)
        reduced = lax.psum_scatter(shaped_sum, "gx", scatter_dimension=1, tiled=True).reshape(
            block_rows, columns
        )
        outputs.append((current_float + reduced).astype(jnp.bfloat16))
        entries.append(jnp.concatenate([key_now, value_now], axis=1))
    return (jnp.stack(outputs), jnp.stack(entries))


def solution(mesh):
    in_specs = (
        P(None, "gx", "yz"),
        P("yz"),
        P("yz", "gx"),
        P("yz", None),
        P("yz", "gx"),
        P("yz", "gx"),
        P("gx", "yz"),
        P("gx", "yz"),
        P(("gx", "yz"), None, None),
        P(("gx", "yz"), None, None),
        P(("gx", "yz")),
    )
    out_specs = (P(None, "gx", "yz"), P(None, ("gx", "yz"), None))
    return jax.shard_map(local, mesh=mesh, in_specs=in_specs, out_specs=out_specs, check_vma=False)
```

profile of v0, /device:TPU:1, one launch (start us, length us, event | category | flops | bytes accessed | tf_op | source)
XLA Modules:
  0.0 459.1 jit_solution(13757767686089250472)
XLA Ops:
  7.2 0.9 fusion.48
  9.5 34.3 %all-reduce = (f32[32]{0:T(128)S(1)}, f32[32]{0:T(128)S(1)}) all-reduce(f32[32]{0:T(128)S(1)} %get-tuple-element.6, f32[32]{0:T(128)S(1)} %get-tuple-element.48), channel_id=1, replica_groups=mesh['gx'=8,'yz'=16] {'yz'}, use_global_device_ids=true, to_apply=%region_7.8 | all-reduce | flops 64 | bytes 512 | tf_op jit(solution)/shard_map/psum | solution.py:93
  44.0 0.8 multiply_convert_fusion.1
  44.9 21.9 %all_gather.12 = bf16[16,16,640]{2,0,1:T(8,128)(2,1)S(1)} all-gather(bf16[16,2,640]{2,0,1:T(8,128)(2,1)S(1)} %copy.36), channel_id=1, replica_groups=mesh['gx'=8,'yz'=16] {'gx'}, dimensions={1}, use_global_device_ids=true | all-gather | bytes 368640 | tf_op jit(solution)/shard_map/all_gather | solution.py:97
  66.8 4.8 %fusion.56 = f32[256,4608]{1,0:T(8,128)S(1)} fusion(bf16[256,640]{1,0:T(8,128)(2,1)S(1)} %bitcast.72, bf16[640,4608]{1,0:T(8,128)(2,1)} %param.15), kind=kOutput, calls=%fused_computation.127 | convolution fusion | flops 1509949440 | bytes 10944512 | tf_op jit(solution)/shard_map/dot_general | solution.py:102
  71.7 2.0 fusion.57
  73.7 0.8 fusion.55
  74.8 4.6 %pad_maximum_fusion = f32[256,11264]{1,0:T(8,128)} fusion(f32[256,512]{1,0:T(8,128)S(1)} %fusion.58, f32[256,4608]{1,0:T(8,128)S(1)} %fusion.57, f32[256,4608]{1,0:T(8,128)S(1)} %fusion.56, f32[256,1536]{1,0:T(8,128)S(1)} %fusion.55), kind=kLoop, calls=%fused_computation | loop fusion | flops 8650752 | bytes 23068672 | tf_op jit(solution)/shard_map/concatenate | solution.py:99
  79.5 12.9 %all_gather.14 = bf16[16,16,640]{2,0,1:T(8,128)(2,1)S(1)} all-gather(bf16[16,2,640]{2,0,1:T(8,128)(2,1)S(1)} %copy.43), channel_id=1, replica_groups=mesh['gx'=8,'yz'=16] {'gx'}, dimensions={1}, use_global_device_ids=true | all-gather | bytes 368640 | tf_op jit(solution)/shard_map/all_gather | solution.py:97
  92.9 2.5 fusion.59
  95.4 4.9 %fusion.60 = f32[256,4608]{1,0:T(8,128)S(1)} fusion(bf16[256,640]{1,0:T(8,128)(2,1)S(1)} %bitcast.78, bf16[640,4608]{1,0:T(8,128)(2,1)} %param.15), kind=kOutput, calls=%fused_computation.131 | convolution fusion | flops 1509949440 | bytes 10944512 | tf_op jit(solution)/shard_map/dot_general | solution.py:102
  100.3 2.0 fusion.61
  102.3 4.8 %pad_maximum_fusion.1 = f32[256,11264]{1,0:T(8,128)} fusion(f32[256,512]{1,0:T(8,128)S(1)} %fusion.62, f32[256,4608]{1,0:T(8,128)S(1)} %fusion.61, f32[256,4608]{1,0:T(8,128)S(1)} %fusion.60, f32[256,1536]{1,0:T(8,128)S(1)} %fusion.59), kind=kLoop, calls=%fused_computation.1 | loop fusion | flops 8650752 | bytes 23068672 | tf_op jit(solution)/shard_map/concatenate | solution.py:99
  108.6 58.2 %reduce-scatter.5.cloned.1.call-done = f32[16,11264]{1,0:T(8,128)} async-done(((f32[256,11264]{1,0:T(8,128)}), f32[16,11264]{1,0:T(8,128)}) %reduce-scatter.5.cloned.1.call-update) | async-done | bytes 720912 | tf_op jit(solution)/shard_map/reduce_scatter | solution.py:98
  166.8 0.8 slice.113
  168.1 94.0 %reduce-scatter.9.cloned.1.call-done = f32[16,11264]{1,0:T(8,128)} async-done(((f32[256,11264]{1,0:T(8,128)}), f32[16,11264]{1,0:T(8,128)}) %reduce-scatter.9.cloned.1.call-update) | async-done | bytes 720912 | tf_op jit(solution)/shard_map/reduce_scatter | solution.py:98
  262.1 0.8 slice.125
  263.5 0.9 slice.172
  265.0 5.4 %all-to-all-start = ((bf16[8,2,1536]{2,1,0:T(2,128)(2,1)}), bf16[8,2,1536]{2,1,0:T(2,128)(2,1)S(1)}, u32[]{:S(2)}, u32[]{:S(2)}) async-start(bf16[8,2,1536]{2,1,0:T(2,128)(2,1)} %all_to_all.48), calls=%async_computation.1 | async-start | bytes 98304 | tf_op jit(solution)/shard_map/all_to_all | solution.py:121
  270.4 0.7 fusion.38
  271.1 4.1 all-to-all-done
  275.4 0.8 fusion.54
  276.6 2.8 fusion.6
  279.3 1.5 all_to_all.50
  280.8 1.5 copy.39
  282.2 4.6 %all-to-all-start.1 = ((bf16[2,8,1536]{2,0,1:T(2,128)(2,1)}), bf16[2,8,1536]{2,0,1:T(2,128)(2,1)}, u32[]{:S(2)}, u32[]{:S(2)}) async-start(bf16[2,8,1536]{2,0,1:T(2,128)(2,1)} %copy.39), calls=%async_computation.2 | async-start | bytes 98304 | tf_op jit(solution)/shard_map/all_to_all | solution.py:138
  286.8 0.7 fusion.18
  287.6 4.2 all-to-all-done.1
  291.8 0.8 all_to_all.53
  292.6 1.6 pad_maximum_fusion.2
  294.9 4.2 all-to-all-start.2
  300.4 3.4 all-to-all-done.2
  304.8 0.8 fusion.52
  305.9 2.1 fusion.12
  309.0 4.0 all-to-all-start.3
  313.1 4.7 %all-to-all-done.3 = bf16[2,8,1536]{2,0,1:T(2,128)(2,1)S(1)} async-done(((bf16[2,8,1536]{2,0,1:T(2,128)(2,1)}), bf16[2,8,1536]{2,0,1:T(2,128)(2,1)S(1)}, u32[]{:S(2)}, u32[]{:S(2)}) %all-to-all-start.3) | async-done | bytes 49184 | tf_op jit(solution)/shard_map/all_to_all | solution.py:138
  318.6 20.6 %all-gather.3.cloned.1.call-done = bf16[256,6144]{1,0:T(8,128)(2,1)} async-done(((bf16[16,6144]{1,0:T(8,128)(2,1)}), bf16[256,6144]{1,0:T(8,128)(2,1)}) %all-gather.3.cloned.1.call-update) | async-done | bytes 3145744 | tf_op jit(solution)/shard_map/all_gather | solution.py:140
  339.2 5.6 %fusion.4 = f32[256,640]{1,0:T(8,128)S(1)} fusion(bf16[4608,640]{1,0:T(8,128)(2,1)} %param.18, bf16[256,6144]{1,0:T(8,128)(2,1)} %all-gather.3.cloned.1.call-done), kind=kOutput, calls=%fused_computation.8 | convolution fusion | flops 1509949440 | bytes 8912896 | tf_op jit(solution)/shard_map/dot_general | solution.py:143
  344.8 1.9 convolution_add_fusion.1
  347.1 1.0 copy.40
  348.2 39.8 %all-gather.5.cloned.1.call-done = bf16[256,6144]{1,0:T(8,128)(2,1)} async-done(((bf16[16,6144]{1,0:T(8,128)(2,1)}), bf16[256,6144]{1,0:T(8,128)(2,1)}) %all-gather.5.cloned.1.call-update) | async-done | bytes 3145744 | tf_op jit(solution)/shard_map/all_gather | solution.py:140
  388.0 5.6 %fusion.2 = f32[256,640]{1,0:T(8,128)S(1)} fusion(bf16[4608,640]{1,0:T(8,128)(2,1)} %param.18, bf16[256,6144]{1,0:T(8,128)(2,1)} %all-gather.5.cloned.1.call-done), kind=kOutput, calls=%fused_computation.6 | convolution fusion | flops 1509949440 | bytes 8912896 | tf_op jit(solution)/shard_map/dot_general | solution.py:143
  393.6 2.0 convolution_add_fusion
  396.0 1.1 copy.49
  397.8 20.2 %reduce-scatter.7.cloned.1.call-done = f32[16,1,2,640]{3,0,2,1:T(8,128)} async-done(((f32[16,8,2,640]{3,0,2,1:T(8,128)}), f32[16,1,2,640]{3,0,2,1:T(8,128)}) %reduce-scatter.7.cloned.1.call-update) | async-done | bytes 81936 | tf_op jit(solution)/shard_map/reduce_scatter | solution.py:145
  418.0 1.0 copy.41
  419.1 31.3 %reduce-scatter.11.cloned.1.call-done = f32[16,1,2,640]{3,0,2,1:T(8,128)} async-done(((f32[16,8,2,640]{3,0,2,1:T(8,128)}), f32[16,1,2,640]{3,0,2,1:T(8,128)}) %reduce-scatter.11.cloned.1.call-update) | async-done | bytes 81936 | tf_op jit(solution)/shard_map/reduce_scatter | solution.py:145
  450.3 1.0 copy.50
  (119 shorter events, 13.9 us)
Async XLA Ops:
  7.2 268.3 %copy-start = (bf16[2,2048,256]{2,1,0:T(8,128)(2,1)S(1)}, bf16[2,2048,256]{2,1,0:T(8,128)(2,1)}, u32[]{:S(2)}) copy-start(bf16[2,2048,256]{2,1,0:T(8,128)(2,1)} %param.19) | copy-start | bytes 6291460
  7.2 159.6 %reduce-scatter.5.cloned.1.call-start = ((), (), s32[]{:S(2)}) async-start(), calls=%async_computation.8 | async-start | bytes 12255232 | tf_op jit(solution)/shard_map/reduce_scatter | solution.py:98
  8.2 0.6 copy-start.7
  8.2 1.3 copy-start.9
  66.7 4.9 %slice-start = ((s8[5898240]{0:T(1024)(128)(4,1)}), s8[4194304]{0:T(1024)(128)(4,1)S(1)}, s32[]{:S(2)}) async-start(s8[5898240]{0:T(1024)(128)(4,1)} %bitcast.68), calls=%async_computation.14 | async-start | bytes 8388608
  66.8 4.8 %slice-start.1 = ((s8[5898240]{0:T(1024)(128)(4,1)}), s8[1703936]{0:T(1024)(128)(4,1)S(1)}, s32[]{:S(2)}) async-start(s8[5898240]{0:T(1024)(128)(4,1)} %bitcast.68), calls=%async_computation.15 | async-start | bytes 3407872
  71.7 2.0 copy-start.1
  71.7 2.8 copy-start.4
  79.5 182.6 %reduce-scatter.9.cloned.1.call-start = ((), (), s32[]{:S(2)}) async-start(), calls=%async_computation.11 | async-start | bytes 12255232 | tf_op jit(solution)/shard_map/reduce_scatter | solution.py:98
  92.9 7.4 %slice-start.2 = ((s8[5898240]{0:T(1024)(128)(4,1)}), s8[4194304]{0:T(1024)(128)(4,1)S(1)}, s32[]{:S(2)}) async-start(s8[5898240]{0:T(1024)(128)(4,1)} %bitcast.70), calls=%async_computation.16 | async-start | bytes 8388608
  95.4 4.9 %slice-start.3 = ((s8[5898240]{0:T(1024)(128)(4,1)}), s8[1703936]{0:T(1024)(128)(4,1)S(1)}, s32[]{:S(2)}) async-start(s8[5898240]{0:T(1024)(128)(4,1)} %bitcast.70), calls=%async_computation.17 | async-start | bytes 3407872
  107.2 0.7 copy-start.15
  265.0 10.2 %all-to-all-start = ((bf16[8,2,1536]{2,1,0:T(2,128)(2,1)}), bf16[8,2,1536]{2,1,0:T(2,128)(2,1)S(1)}, u32[]{:S(2)}, u32[]{:S(2)}) async-start(bf16[8,2,1536]{2,1,0:T(2,128)(2,1)} %all_to_all.48), calls=%async_computation.1 | async-start | bytes 98304 | tf_op jit(solution)/shard_map/all_to_all | solution.py:121
  271.1 15.7 %copy-start.6 = (f32[16,11264]{1,0:T(8,128)S(1)}, f32[16,11264]{1,0:T(8,128)}, u32[]{:S(2)}) copy-start(f32[16,11264]{1,0:T(8,128)} %reduce-scatter.5.cloned.1.call-done) | copy-start | bytes 2162692
  275.4 18.8 %copy-start.5 = (f32[16,11264]{1,0:T(8,128)S(1)}, f32[16,11264]{1,0:T(8,128)}, u32[]{:S(2)}) copy-start(f32[16,11264]{1,0:T(8,128)} %reduce-scatter.9.cloned.1.call-done) | copy-start | bytes 2162692
  282.2 9.5 %all-to-all-start.1 = ((bf16[2,8,1536]{2,0,1:T(2,128)(2,1)}), bf16[2,8,1536]{2,0,1:T(2,128)(2,1)}, u32[]{:S(2)}, u32[]{:S(2)}) async-start(bf16[2,8,1536]{2,0,1:T(2,128)(2,1)} %copy.39), calls=%async_computation.2 | async-start | bytes 98304 | tf_op jit(solution)/shard_map/all_to_all | solution.py:138
  286.8 52.4 %all-gather.3.cloned.1.call-start = ((), (), s32[]{:S(2)}) async-start(), calls=%async_computation.9 | async-start | bytes 3342336 | tf_op jit(solution)/shard_map/all_gather | solution.py:140
  294.9 9.0 %all-to-all-start.2 = ((bf16[8,2,1536]{2,1,0:T(2,128)(2,1)}), bf16[8,2,1536]{2,1,0:T(2,128)(2,1)S(1)}, u32[]{:S(2)}, u32[]{:S(2)}) async-start(bf16[8,2,1536]{2,1,0:T(2,128)(2,1)} %all_to_all.54), calls=%async_computation.5 | async-start | bytes 98304 | tf_op jit(solution)/shard_map/all_to_all | solution.py:121
  309.0 8.8 %all-to-all-start.3 = ((bf16[2,8,1536]{2,0,1:T(2,128)(2,1)}), bf16[2,8,1536]{2,0,1:T(2,128)(2,1)S(1)}, u32[]{:S(2)}, u32[]{:S(2)}) async-start(bf16[2,8,1536]{2,0,1:T(2,128)(2,1)} %copy.48), calls=%async_computation.6 | async-start | bytes 98304 | tf_op jit(solution)/shard_map/all_to_all | solution.py:138
  313.0 75.0 %all-gather.5.cloned.1.call-start = ((), (), s32[]{:S(2)}) async-start(), calls=%async_computation.12 | async-start | bytes 3342336 | tf_op jit(solution)/shard_map/all_gather | solution.py:140
  318.6 99.4 %reduce-scatter.7.cloned.1.call-start = ((), (), s32[]{:S(2)}) async-start(), calls=%async_computation.10 | async-start | bytes 737280 | tf_op jit(solution)/shard_map/reduce_scatter | solution.py:145
  339.2 5.6 %copy-start.2 = (bf16[1536,640]{1,0:T(8,128)(2,1)S(1)}, bf16[1536,640]{1,0:T(8,128)(2,1)}, u32[]{:S(2)}) copy-start(bf16[1536,640]{1,0:T(8,128)(2,1)} %param.17) | copy-start | bytes 5898244
  348.2 102.1 %reduce-scatter.11.cloned.1.call-start = ((), (), s32[]{:S(2)}) async-start(), calls=%async_computation.13 | async-start | bytes 737280 | tf_op jit(solution)/shard_map/reduce_scatter | solution.py:145
  388.0 5.6 %copy-start.3 = (bf16[1536,640]{1,0:T(8,128)(2,1)S(1)}, bf16[1536,640]{1,0:T(8,128)(2,1)}, u32[]{:S(2)}) copy-start(bf16[1536,640]{1,0:T(8,128)(2,1)} %param.17) | copy-start | bytes 5898244
  393.6 3.5 copy-start.11
  393.6 3.5 copy-start.12
  393.6 3.5 copy-start.13
  393.6 3.5 copy-start.14
  393.6 25.3 %copy-start.10 = (bf16[1,32,640]{2,1,0:T(8,128)(2,1)S(1)}, bf16[1,32,640]{2,1,0:T(8,128)(2,1)}, u32[]{:S(2)}) copy-start(bf16[1,32,640]{2,1,0:T(8,128)(2,1)} %copy-done.9) | copy-start | bytes 122884
  393.6 57.7 %copy-start.8 = (bf16[1,32,640]{2,1,0:T(8,128)(2,1)S(1)}, bf16[1,32,640]{2,1,0:T(8,128)(2,1)}, u32[]{:S(2)}) copy-start(bf16[1,32,640]{2,1,0:T(8,128)(2,1)} %copy-done.7) | copy-start | bytes 122884
Sparse Core Ops, SparseCore 0:
  79.6 87.1 reduce-scatter.4
  170.7 91.4 reduce-scatter.8
  294.3 44.8 all-gather.2
  341.2 46.7 all-gather.4
  390.2 27.6 reduce-scatter.6
  420.2 30.0 reduce-scatter.10
where the time goes:
time: 462 us; the launch traced here: 459 us
  waiting for transfers between devices  280 us (61%)
  blocking collectives  69 us (15%)
  matrix products  39.7 us (9%)
  other arithmetic  19.9 us (4%)
  starting transfers between devices  18.3 us (4%)
  local copies, waits for them, and re-layouts  17 us (4%)
  between operations  14.7 us (3%)
    reduce_scatter x2, waiting for transfers between devices, local(): lax.psum_scatter(jnp.concatenate([jnp.dot(gathered, w_query, preferred_el...  152 us
    all_gather x2, waiting for transfers between devices, local(): piece_rows = lax.all_gather(joined, 'yz', axis=0, tiled=True)  60.4 us
    reduce_scatter x2, waiting for transfers between devices, local(): lax.psum_scatter(shaped_sum, 'gx', scatter_dimension=1, tiled=True)  51.5 us
    all_gather x2, blocking collectives, local(): lax.all_gather(shaped, 'gx', axis=1, tiled=True)  34.8 us
    psum x1, blocking collectives, local(): square_total = lax.psum(squares, 'yz')  34.3 us
    dot_general x2, matrix products, local(): jnp.dot(piece_rows[:, query_cols:], w_down, preferred_element_type=jnp.fl...  11.1 us
    dot_general x2, matrix products, local(): jnp.dot(gathered, w_gate, preferred_element_type=jnp.float32)  9.71 us
    all_to_all x2, starting transfers between devices, local(): lax.all_to_all(query_block, 'gx', split_axis=0, concat_axis=1, tiled=True)  9.55 us
  transfers between devices with their start and end apart: 10, of which 10 were waited for; matrix products, arithmetic and copies ran while one was open for 10% of the time, Pallas kernels for 0%

commit v1 on v0

v1 whole, which is shorter than its diff:
```python
import functools
import math

import jax
import jax.numpy as jnp
from jax import lax
from jax.experimental import pallas as pl
from jax.experimental.pallas import tpu as pltpu
from jax.sharding import PartitionSpec as P

EPSILON = 1e-06
MESH = pl.DeviceIdType.MESH
BF = jnp.bfloat16
F32 = jnp.float32
HIDDEN_CHUNKS = (768, 768, 768)
RING = 4


def dot(a, b):
    return jnp.dot(a, b, preferred_element_type=F32)


def dot_t(a, b):
    return lax.dot_general(a, b, (((1,), (1,)), ((), ())), preferred_element_type=F32)


def iota(shape, dim):
    return lax.broadcasted_iota(jnp.int32, shape, dim)


def one_hot(mask):
    return jnp.where(mask, 1.0, 0.0).astype(BF)


def add_f32(*terms):
    total = terms[0].astype(F32)
    for term in terms[1:]:
        total = total + term.astype(F32)
    return total


class Scratch:
    def __init__(self):
        self.names, self.shapes = [], []

    def add(self, name, shape, dtype=BF):
        self.names.append(name)
        self.shapes.append(pltpu.VMEM(shape, dtype))


def query_width(f):
    return 768 + 128 * f


def scratch_plan(columns):
    s = Scratch()
    for f in range(2):
        for k in range(1 + len(HIDDEN_CHUNKS)):
            hc = 768 if k == 0 else HIDDEN_CHUNKS[k - 1]
            w = query_width(f) if k == 0 else 2 * hc
            t = (k, f)
            s.add(("w1",) + t, (columns, w))
            s.add(("part",) + t, (4, 4, 32, w))
            s.add(("r1",) + t, (2, 2, 32, w))
            s.add(("r2",) + t, (2, 4, 32, w))
            s.add(("q1",) + t, (2, 16, w))
            s.add(("q2",) + t, (2, 32, w))
            s.add(("ag",) + t, (4, 4, 32, hc))
            s.add(("w2",) + t, (hc, columns))
    s.add("keys", (2, 2048, 256))
    s.add("values", (2, 2048, 256))
    s.add("tk", (8, 64, columns))
    s.add("xs", (2, 512, columns))
    s.add("acc", (512, columns), F32)
    s.add("ob", (2, 4, 64, columns))
    s.add("fr", (4, 64, columns))
    s.add("fz1", (2, 32, columns))
    s.add("fz2", (2, 64, columns))
    s.add("qsend", (8, 32, 256))
    s.add("qrecv", (8, 32, 256))
    s.add("asend", (8, 32, 256))
    s.add("arecv", (8, 32, 256))
    s.add("inv", (32, 128), F32)
    return s


class Half:
    pass


def kernel(
    plan_names,
    model_width,
    tok,
    gain,
    wq,
    wsh,
    wg,
    wu,
    wo,
    wd,
    kc,
    vc,
    lens,
    cos_ref,
    sin_ref,
    out,
    entries,
    *scratch,
):
    n = len(plan_names)
    b = dict(zip(plan_names, scratch[:n]))
    send_sem, recv_sem, local_sem = scratch[n:]
    columns = tok.shape[1]
    g = lax.axis_index("gx")
    q = lax.axis_index("yz")
    z, c = g // 2, lax.rem(g, 2)
    y, x = q // 4, lax.rem(q, 4)

    def step(v, d):
        return lax.rem(v + d + RING, RING)

    def at_x(d):
        return (g, y * 4 + step(x, d))

    def at_y(d):
        return (g, step(y, d) * 4 + x)

    def at_z(d):
        return (step(z, d) * 2 + c, q)

    partner = (z * 2 + 1 - c, q)

    started = []

    def rc(src, dst, dev):
        i = len(started)
        cp = pltpu.make_async_remote_copy(
            src_ref=src,
            dst_ref=dst,
            send_sem=send_sem.at[i],
            recv_sem=recv_sem.at[i],
            device_id=dev,
            device_id_type=MESH,
        )
        cp.start()
        started.append(cp)
        return cp

    loads = {}

    def load(name, src, dst):
        i = sum(len(v) for v in loads.values())
        cp = pltpu.make_async_copy(src, dst, local_sem.at[i])
        cp.start()
        loads.setdefault(name, []).append(cp)

    def loaded(name):
        for cp in loads[name]:
            cp.wait()

    load("tok", tok, b["tk"].at[g])
    shared_at = pl.multiple_of(z * 128, 128)
    load(("w1", 0, 1), wq.at[:, 768:1536], b["w1", 0, 1].at[:, 0:768])
    load(("w1", 0, 1), wsh.at[:, pl.ds(shared_at, 128)], b["w1", 0, 1].at[:, 768:896])
    load(("w1", 0, 0), wq.at[:, 0:768], b["w1", 0, 0])
    hidden_at = {}
    base = 0
    for k, hc in enumerate(HIDDEN_CHUNKS, 1):
        for f in range(2):
            hidden_at[k, f] = base
            base += hc

    def load_w1(k):
        hc = HIDDEN_CHUNKS[k - 1]
        for f in range(2):
            at = hidden_at[k, f]
            load(("w1", k, f), wg.at[:, at : at + hc], b["w1", k, f].at[:, 0:hc])
            load(("w1", k, f), wu.at[:, at : at + hc], b["w1", k, f].at[:, hc : 2 * hc])

    barrier = pltpu.get_barrier_semaphore()
    others = [lax.rem(g + d, 8) for d in range(1, 8)]
    peers = [at_x(1), at_x(-1), at_y(1), at_y(-1)] + [(o, q) for o in others]
    for peer in peers:
        pl.semaphore_signal(barrier, inc=1, device_id=peer, device_id_type=MESH)
    loaded("tok")
    pl.semaphore_wait(barrier, len(peers))

    tk = b["tk"]

    def block(zz):
        return zz * 2 + c

    zr, zl, zo = step(z, 1), step(z, -1), step(z, 2)
    own = tk.at[g]
    t_r = rc(own, own, at_z(1))
    t_l = rc(own, own, at_z(-1))
    pairs = [rc(own, own, partner)]
    for k in range(1, 1 + len(HIDDEN_CHUNKS)):
        load_w1(k)
    t_r.wait_recv()
    blk = tk.at[block(zl), 0:32]
    f_r = rc(blk, blk, at_z(1))
    blk = tk.at[block(zl)]
    pairs.append(rc(blk, blk, partner))
    t_l.wait_recv()
    blk = tk.at[block(zr), 32:64]
    f_l = rc(blk, blk, at_z(-1))
    blk = tk.at[block(zr)]
    pairs.append(rc(blk, blk, partner))
    f_r.wait_recv()
    f_l.wait_recv()
    blk = tk.at[block(zo)]
    pairs.append(rc(blk, blk, partner))
    for k in range(1 + len(HIDDEN_CHUNKS)):
        for f in range(2):
            if k == 0:
                load(("w2", k, f), wo.at[768 * f : 768 * f + 768], b["w2", k, f])
            else:
                at = hidden_at[k, f]
                load(("w2", k, f), wd.at[at : at + HIDDEN_CHUNKS[k - 1]], b["w2", k, f])
    load("kv", kc, b["keys"])
    load("kv", vc, b["values"])
    for cp in pairs:
        cp.wait_recv()

    tokens_all = tk[...].reshape(512, columns)
    row_i, col_i = iota((512, 512), 0), iota((512, 512), 1)
    tail = (((row_i >> 2) & 7) << 6) | (((row_i >> 1) & 1) << 5) | (row_i & 1)
    d1, d2 = (row_i >> 7) & 3, (row_i >> 5) & 3
    source = {0: tail | (d2 << 3) | (d1 << 1), 1: tail | (d1 << 3) | (d2 << 1)}
    squares = None
    gain_row = gain[...]
    for f in (1, 0):
        rows = dot(one_hot(source[f] == col_i), tokens_all)
        if f == 1:
            squares = jnp.sum(rows * rows, axis=1, keepdims=True)
        b["xs"][f] = (rows * gain_row).astype(BF)

    lane = iota((1, 128), 1)
    mine = (lane >> 6) == c
    spread = 1.0 + (lane & 63).astype(F32) * (1.0 / 64.0)

    halves = {}
    for f in range(2):
        h = Half()
        first, second = (at_x, at_y) if f == 0 else (at_y, at_x)
        p1, p2 = (x, y) if f == 0 else (y, x)
        h.first, h.second, h.p1, h.p2 = first, second, p1, p2
        h.r1, h.l1, h.o1 = step(p1, 1), step(p1, -1), step(p1, 2)
        h.r2, h.l2, h.o2 = step(p2, 1), step(p2, -1), step(p2, 2)
        halves[f] = h
    cps = {}

    def product(k, f):
        loaded(("w1", k, f))
        part, w1 = b["part", k, f], b["w1", k, f]
        w = 768 if k == 0 else w1.shape[1]

        @pl.loop(0, w // 256)
        def _(i):
            at = pl.ds(pl.multiple_of(i * 256, 256), 256)
            value = dot(b["xs"][f], w1[:, at]).astype(BF)
            part[:, :, :, at] = value.reshape(4, 4, 32, 256)

        if k == 0 and f == 1:
            value = dot(b["xs"][f], w1[:, 768:896])
            value = jnp.where(mine, value, squares * spread).astype(BF)
            part[:, :, :, 768:896] = value.reshape(4, 4, 32, 128)

    def s1(k, f):
        h, part, r1, r2 = halves[f], b["part", k, f], b["r1", k, f], b["r2", k, f]
        cps[k, f] = [
            rc(part.at[h.o1, 0:2], r1.at[0], h.first(1)),
            rc(part.at[h.o1, 2:4], r1.at[1], h.first(-1)),
            rc(part.at[h.r1, 2:4], r2.at[0, 2:4], h.first(1)),
            rc(part.at[h.l1, 0:2], r2.at[1, 0:2], h.first(-1)),
        ]

    def s2(k, f):
        h, part, r1, r2 = halves[f], b["part", k, f], b["r1", k, f], b["r2", k, f]
        one, two, three, four = cps[k, f]
        one.wait_recv()
        part[h.r1, 0:2] = add_f32(part[h.r1, 0:2], r1[0]).astype(BF)
        five = rc(part.at[h.r1, 0:2], r2.at[0, 0:2], h.first(1))
        two.wait_recv()
        part[h.l1, 2:4] = add_f32(part[h.l1, 2:4], r1[1]).astype(BF)
        six = rc(part.at[h.l1, 2:4], r2.at[1, 2:4], h.first(-1))
        cps[k, f] = [three, four, five, six]

    def s3(k, f):
        h, part, r2 = halves[f], b["part", k, f], b["r2", k, f]
        q1, q2 = b["q1", k, f], b["q2", k, f]
        for cp in cps[k, f]:
            cp.wait_recv()

        def total(d):
            part[h.p1, d] = add_f32(part[h.p1, d], r2[0, d], r2[1, d]).astype(BF)

        total(h.o2)
        new = [
            rc(part.at[h.p1, h.o2, 0:16], q1.at[0], h.second(1)),
            rc(part.at[h.p1, h.o2, 16:32], q1.at[1], h.second(-1)),
        ]
        total(h.r2)
        new.append(rc(part.at[h.p1, h.r2, 16:32], q2.at[0, 16:32], h.second(1)))
        total(h.l2)
        new.append(rc(part.at[h.p1, h.l2, 0:16], q2.at[1, 0:16], h.second(-1)))
        total(h.p2)
        cps[k, f] = new

    def s4(k, f):
        h, part = halves[f], b["part", k, f]
        q1, q2 = b["q1", k, f], b["q2", k, f]
        one, two, three, four = cps[k, f]
        one.wait_recv()
        part[h.p1, h.r2, 0:16] = add_f32(part[h.p1, h.r2, 0:16], q1[0]).astype(BF)
        five = rc(part.at[h.p1, h.r2, 0:16], q2.at[0, 0:16], h.second(1))
        two.wait_recv()
        part[h.p1, h.l2, 16:32] = add_f32(part[h.p1, h.l2, 16:32], q1[1]).astype(BF)
        six = rc(part.at[h.p1, h.l2, 16:32], q2.at[1, 16:32], h.second(-1))
        cps[k, f] = [three, four, five, six]

    def s5(k, f, lo, hi):
        h, part, q2 = halves[f], b["part", k, f], b["q2", k, f]
        return add_f32(part[h.p1, h.p2, :, lo:hi], q2[0, :, lo:hi], q2[1, :, lo:hi])

    def s5_wait(k, f):
        for cp in cps[k, f]:
            cp.wait_recv()

    def hidden(k, f):
        s5_wait(k, f)
        h, hc = halves[f], HIDDEN_CHUNKS[k - 1]
        inv = b["inv"][:, 0:1]
        gate = s5(k, f, 0, hc) * inv
        up = s5(k, f, hc, 2 * hc) * inv
        value = gate * (1.0 / (1.0 + jnp.exp(-gate))) * up
        b["ag", k, f][h.p2, h.p1] = value.astype(BF)

    def g1(k, f):
        h, ag = halves[f], b["ag", k, f]
        blk = ag.at[h.p2, h.p1]
        cps["g", k, f] = [rc(blk, blk, h.first(1)), rc(blk, blk, h.first(-1))]

    def g2(k, f):
        h, ag = halves[f], b["ag", k, f]
        one, two = cps["g", k, f]
        one.wait_recv()
        blk = ag.at[h.p2, h.l1, 0:16]
        three = rc(blk, blk, h.first(1))
        two.wait_recv()
        blk = ag.at[h.p2, h.r1, 16:32]
        four = rc(blk, blk, h.first(-1))
        cps["g", k, f] = [three, four]

    def g3(k, f):
        h, ag = halves[f], b["ag", k, f]
        for cp in cps["g", k, f]:
            cp.wait_recv()
        blk = ag.at[h.p2]
        cps["g", k, f] = [rc(blk, blk, h.second(1)), rc(blk, blk, h.second(-1))]

    def g4(k, f):
        h, ag = halves[f], b["ag", k, f]
        one, two = cps["g", k, f]
        one.wait_recv()
        blk = ag.at[h.l2, 0:2]
        three = rc(blk, blk, h.second(1))
        two.wait_recv()
        blk = ag.at[h.r2, 2:4]
        four = rc(blk, blk, h.second(-1))
        cps["g", k, f] = [three, four]

    first_product = [True]

    def second(k, f):
        for cp in cps["g", k, f]:
            cp.wait_recv()
        loaded(("w2", k, f))
        ag, w2, acc = b["ag", k, f], b["w2", k, f], b["acc"]
        start = first_product[0]
        first_product[0] = False
        for lo, hi in ((0, 256), (256, 512), (512, columns)):
            value = dot(ag[...].reshape(512, ag.shape[3]), w2[:, lo:hi])
            if start:
                acc[:, lo:hi] = value
            elif f == 0:
                acc[:, lo:hi] += value
            else:
                for yy in range(4):
                    for xx in range(4):
                        to, frm = (yy * 4 + xx) * 32, (xx * 4 + yy) * 32
                        acc[to : to + 32, lo:hi] += value[frm : frm + 32]

    def exchange(send, recv):
        done = []
        for o in others:
            done.append(rc(send.at[o], recv.at[g], (o, q)))
        recv[g] = send[g]
        return done

    def spread_rows(head):
        row, col = iota((256, 32), 0), iota((256, 32), 1)
        return one_hot((col == (((row >> 5) << 2) | (row & 3))) & (((row >> 2) & 7) == head))

    def collect_rows(head):
        row, col = iota((32, 256), 0), iota((32, 256), 1)
        return one_hot((row == (((col >> 5) << 2) | (col & 3))) & (((col >> 2) & 7) == head))

    def query_out():
        s5_wait(0, 0)
        s5_wait(0, 1)
        shared = s5(0, 1, 768, 896)
        total = jnp.sum(jnp.where(mine, 0.0, shared), axis=1, keepdims=True) * (1.0 / 95.5)
        inv = lax.rsqrt(total / model_width + EPSILON)
        b["inv"][...] = jnp.broadcast_to(inv, (32, 128))
        shared = jnp.where(mine, shared * inv, 0.0)
        low = lax.rem(z, 2) == 0
        shared = jnp.concatenate([jnp.where(low, shared, 0.0), jnp.where(low, 0.0, shared)], axis=1)
        rows = dot(spread_rows(6), shared.astype(BF))
        for f in range(2):
            for i in range(3):
                piece = (s5(0, f, i * 256, i * 256 + 256) * inv).astype(BF)
                rows = rows + dot(spread_rows(f * 3 + i), piece)
        b["qsend"][...] = rows.astype(BF).reshape(8, 32, 256)
        cps["q"] = exchange(b["qsend"], b["qrecv"])

    def rotate(rows):
        count = rows.shape[0]
        rows = rows.reshape(count // 8, 8, 256)
        front, back = rows[:, :, :128], rows[:, :, 128:]
        cosine, sine = cos_ref[...][None], sin_ref[...][None]
        return jnp.concatenate(
            [front * cosine - back * sine, back * cosine + front * sine], axis=2
        ).reshape(count, 256)

    def attention():
        for cp in cps["q"]:
            cp.wait_recv()
        loaded("kv")
        raw = b["qrecv"][...].reshape(256, 256)
        queries = rotate(raw.astype(F32)).astype(BF)
        row, col = iota((128, 256), 0), iota((128, 256), 1)
        pick = (row < 4) & ((col & 31) == row + 24)
        key_now = rotate(dot(one_hot(pick & (col < 128)), raw)).astype(BF)
        value_now = dot(one_hot(pick & (col >= 128)), raw).astype(BF)
        fresh = jnp.concatenate([key_now[0:8], value_now[0:8]], axis=1)
        entries[...] = fresh
        result = None
        for j in range(2):
            chosen = one_hot(col == (((row >> 4) << 5) + ((row & 15) << 1) + j))
            heads = dot(chosen, queries).astype(BF)
            scores = dot_t(heads, b["keys"][j]) * (1.0 / 16.0)
            live = iota(scores.shape, 1) < lens[j]
            scores = jnp.where(live, scores, -jnp.inf)
            now = dot_t(heads, key_now) * (1.0 / 16.0)
            r, n_ = iota((128, 128), 0), iota((128, 128), 1)
            now = jnp.where((n_ < 4) & ((n_ & 1) == j) & ((n_ >> 1) <= (r & 1)), now, -jnp.inf)
            top = jnp.maximum(
                jnp.max(scores, axis=1, keepdims=True), jnp.max(now, axis=1, keepdims=True)
            )
            scores = jnp.exp(scores - top)
            now = jnp.exp(now - top)
            under = jnp.sum(scores, axis=1, keepdims=True) + jnp.sum(now, axis=1, keepdims=True)
            scale = 1.0 / under
            mixed = dot((scores * scale).astype(BF), b["values"][j]) + dot(
                (now * scale).astype(BF), value_now
            )
            brow, bcol = iota((256, 128), 0), iota((256, 128), 1)
            back = one_hot(brow == (((bcol >> 4) << 5) + ((bcol & 15) << 1) + j))
            term = dot(back, mixed.astype(BF))
            result = term if result is None else result + term
        b["asend"][...] = result.astype(BF).reshape(8, 32, 256)
        cps["a"] = exchange(b["asend"], b["arecv"])

    def attended():
        for cp in cps["a"]:
            cp.wait_recv()
        raw = b["arecv"][...].reshape(256, 256)
        for f in range(2):
            h = halves[f]
            for i in range(3):
                value = dot(collect_rows(f * 3 + i), raw).astype(BF)
                b["ag", 0, f][h.p2, h.p1, :, i * 256 : i * 256 + 256] = value

    def both(stage, k):
        for f in (1, 0) if k == 0 else (0, 1):
            stage(k, f)

    def start(k):
        for f in (1, 0) if k == 0 else (0, 1):
            product(k, f)
            s1(k, f)

    start(0)
    start(1)
    both(s2, 0)
    both(s3, 0)
    both(s2, 1)
    both(s4, 0)
    start(2)
    both(s3, 1)
    query_out()
    both(s2, 2)
    both(s4, 1)
    start(3)
    attention()
    both(s3, 2)
    both(hidden, 1)
    both(g1, 1)
    both(s2, 3)
    both(s4, 2)
    attended()
    both(g1, 0)
    both(g2, 1)
    both(s3, 3)
    both(hidden, 2)
    both(g1, 2)
    both(g3, 1)
    both(g2, 0)
    both(s4, 3)
    both(g2, 2)
    both(g3, 0)
    both(g4, 1)
    both(hidden, 3)
    both(g1, 3)
    both(g3, 2)
    both(g4, 0)
    both(g2, 3)
    both(second, 1)
    both(g3, 3)
    both(g4, 2)
    both(second, 0)
    both(g4, 3)
    both(second, 2)
    both(second, 3)

    row_o, col_o = iota((512, 512), 0), iota((512, 512), 1)
    gx_o = (((row_o >> 6) & 3) << 1) | (row_o >> 8)
    wanted = (((row_o >> 1) & 15) << 5) | (gx_o << 2) | (((row_o >> 5) & 1) << 1) | (row_o & 1)
    moved = dot(one_hot(wanted == col_o), b["acc"][...].astype(BF)).astype(BF)
    ob, fr, fz1, fz2 = b["ob"], b["fr"], b["fz1"], b["fz2"]
    ob[...] = moved.reshape(2, 4, 64, columns)
    cp = rc(ob.at[1 - c], fr, partner)
    cp.wait_recv()

    def add_partner(zz):
        ob[c, zz] = add_f32(ob[c, zz], fr[zz]).astype(BF)

    add_partner(zo)
    one = rc(ob.at[c, zo, 0:32], fz1.at[0], at_z(1))
    two = rc(ob.at[c, zo, 32:64], fz1.at[1], at_z(-1))
    add_partner(zr)
    three = rc(ob.at[c, zr, 32:64], fz2.at[0, 32:64], at_z(1))
    add_partner(zl)
    four = rc(ob.at[c, zl, 0:32], fz2.at[1, 0:32], at_z(-1))
    one.wait_recv()
    ob[c, zr, 0:32] = add_f32(ob[c, zr, 0:32], fz1[0]).astype(BF)
    five = rc(ob.at[c, zr, 0:32], fz2.at[0, 0:32], at_z(1))
    two.wait_recv()
    ob[c, zl, 32:64] = add_f32(ob[c, zl, 32:64], fz1[1]).astype(BF)
    six = rc(ob.at[c, zl, 32:64], fz2.at[1, 32:64], at_z(-1))
    mine_sum = add_f32(b["tk"][g], ob[c, z], fr[z])
    for cp in (three, four, five, six):
        cp.wait_recv()
    out[...] = (mine_sum + fz2[0].astype(F32) + fz2[1].astype(F32)).astype(BF)
    for cp in started:
        cp.wait_send()


def local(
    tokens,
    norm_gain,
    w_query,
    w_shared,
    w_gate,
    w_up,
    w_out,
    w_down,
    key_cache,
    value_cache,
    lengths,
):
    steps, block_rows, columns = tokens.shape
    model_width = columns * lax.axis_size("yz")
    rows = jnp.arange(8)
    positions = (lengths[rows % 2] + (rows // 2) % 2).astype(F32)
    frequency = jnp.exp(jnp.arange(128, dtype=F32) * (-2.0 * math.log(10000.0) / 256))
    angles = positions[:, None] * frequency
    plan = scratch_plan(columns)
    hbm = pl.BlockSpec(memory_space=pl.ANY)
    vmem = pl.BlockSpec(memory_space=pltpu.VMEM)
    smem = pl.BlockSpec(memory_space=pltpu.SMEM)
    copies = 256
    layer, entries = pl.pallas_call(
        functools.partial(kernel, plan.names, model_width),
        out_shape=(
            jax.ShapeDtypeStruct((steps * block_rows, columns), BF),
            jax.ShapeDtypeStruct((8, 512), BF),
        ),
        in_specs=[hbm, vmem] + [hbm] * 8 + [smem, vmem, vmem],
        out_specs=(vmem, vmem),
        scratch_shapes=plan.shapes
        + [
            pltpu.SemaphoreType.DMA((copies,)),
            pltpu.SemaphoreType.DMA((copies,)),
            pltpu.SemaphoreType.DMA((48,)),
        ],
        compiler_params=pltpu.CompilerParams(
            collective_id=0, has_side_effects=True, vmem_limit_bytes=64 << 20
        ),
        cost_estimate=pl.CostEstimate(
            flops=12 * 10**9, bytes_accessed=28 * 10**6, transcendentals=10**6
        ),
    )(
        tokens.reshape(steps * block_rows, columns),
        norm_gain[None],
        w_query,
        w_shared,
        w_gate,
        w_up,
        w_out,
        w_down,
        key_cache,
        value_cache,
        lengths,
        jnp.cos(angles),
        jnp.sin(angles),
    )
    return layer.reshape(steps, block_rows, columns), entries[:4].reshape(2, 2, 512)


def solution(mesh):
    in_specs = (
        P(None, "gx", "yz"),
        P("yz"),
        P("yz", "gx"),
        P("yz", None),
        P("yz", "gx"),
        P("yz", "gx"),
        P("gx", "yz"),
        P("gx", "yz"),
        P(("gx", "yz"), None, None),
        P(("gx", "yz"), None, None),
        P(("gx", "yz")),
    )
    out_specs = (P(None, "gx", "yz"), P(None, ("gx", "yz"), None))
    return jax.shard_map(local, mesh=mesh, in_specs=in_specs, out_specs=out_specs, check_vma=False)
```

time: 462 us -> 138 us (0.30)
  waiting for transfers between devices: 280 us -> 0 us
  Pallas kernels: 0 us -> 131 us
  blocking collectives: 69 us -> 0 us
  matrix products: 39.7 us -> 0 us
  other arithmetic: 19.9 us -> 0.75 us
  starting transfers between devices: 18.3 us -> 0 us
  between operations: 14.7 us -> 0.65 us
  local copies, waits for them, and re-layouts: 17 us -> 5.41 us
    reduce_scatter x4 -> x0, waiting for transfers between devices: 204 us -> none  [the longest x2 152 us: local(): lax.psum_scatter(jnp.concatenate([jnp.dot(gathered, w_query, preferred_el...]
    pallas_call x0 -> x1, Pallas kernels: none -> 131 us  [local(): pl.pallas_call(functools.partial(kernel, plan.names, model_width), out_sh...]
    all_gather x2 -> x0, waiting for transfers between devices: 60.4 us -> none  [local(): piece_rows = lax.all_gather(joined, 'yz', axis=0, tiled=True)]
    dot_general x19 -> x0, matrix products: 39.7 us -> none  [the longest x2 11.1 us: local(): jnp.dot(piece_rows[:, query_cols:], w_down, preferred_element_type=jnp.fl...]
    all_gather x2 -> x0, blocking collectives: 34.8 us -> none  [local(): lax.all_gather(shaped, 'gx', axis=1, tiled=True)]
    psum x1 -> x0, blocking collectives: 34.3 us -> none  [local(): square_total = lax.psum(squares, 'yz')]
    all_to_all x4 -> x0, starting transfers between devices: 18.1 us -> none  [the longest x2 9.55 us: local(): lax.all_to_all(query_block, 'gx', split_axis=0, concat_axis=1, tiled=True)]
    all_to_all x4 -> x0, waiting for transfers between devices: 16.4 us -> none  [the longest x2 8.87 us: local(): lax.all_to_all(attended, 'gx', split_axis=1, concat_axis=0, tiled=True)]
  transfers between devices with their start and end apart: 10 -> 0, of which waited for: 10 -> 0; matrix products, arithmetic and copies ran while one was open for 10% -> 0% of each run, Pallas kernels for 0% -> 0%
where the time goes in v1:
time: 138 us
  Pallas kernels  131 us (95%)
  local copies, waits for them, and re-layouts  5.41 us (4%)
    pallas_call x1, Pallas kernels, local(): pl.pallas_call(functools.partial(kernel, plan.names, model_width), out_sh...  131 us

profile of v1, /device:TPU:1, one launch (start us, length us, event | category | flops | bytes accessed | tf_op | source)
XLA Modules:
  0.0 138.0 jit_solution(1650356392167608027)
XLA Ops:
  0.7 1.3 broadcast_in_dim.2.gain
  1.9 1.3 gather_fusion
  3.2 0.7 multiply_sine_fusion
  4.0 131.2 %shard_map.122 = (bf16[64,640]{1,0:T(8,128)(2,1)}, bf16[8,512]{1,0:T(8,128)(2,1)}) custom-call(bf16[64,640]{1,0:T(8,128)(2,1)} %bitcast.5, f32[1,640]{1,0:T(1,128)} %broadcast_in_dim.2.gain, bf16[640,1536]{1,0:T(8,128)(2,1)} %wq.1, bf16[640,512]{1,0:T(8,128)(2,1)} %wsh.1, bf16[640,4608]{1,0:T(8,128)(2,1)} %wg.1, bf16[640,4608]{1,0:T(8,128)(2,1)} %wu.1, ...), custom_call_target="tpu_custom_call" | custom-call | flops 12000000000 | bytes 28000000 | tf_op jit(solution)/shard_map/pallas_call | solution.py:596
  135.1 0.7 slice.3
  135.8 0.6 reshape.79
  136.4 1.5 %copy.14 = bf16[2,32,640]{2,1,0:T(8,128)(2,1)} copy(bf16[2,32,640]{2,1,0:T(8,128)(2,1)} %bitcast.4) | data formatting | bytes 163840
  (4 shorter events, 0.0 us)

commit v2 on v1

v2 whole, which is shorter than its diff:
```python
import functools
import math

import jax
import jax.numpy as jnp
import numpy as np
from jax import lax
from jax.experimental import pallas as pl
from jax.experimental.pallas import tpu as pltpu
from jax.sharding import PartitionSpec as P

EPSILON = 1e-06
MESH = pl.DeviceIdType.MESH
BF = jnp.bfloat16
F32 = jnp.float32
HIDDEN_CHUNKS = (768, 768, 768)
RING = 4
ORDER = (
    ("product", 0, 1),
    ("s1", 0, 1),
    ("ordered", 0, 0),
    ("product", 0, 0),
    ("s1", 0, 0),
    ("more_loads", 0, 0),
    ("product", 1, 1),
    ("s2", 0, 1),
    ("s1", 1, 1),
    ("s2", 0, 0),
    ("product", 1, 0),
    ("s1", 1, 0),
    ("product", 3, 1),
    ("s3", 0, 0),
    ("product", 2, 0),
    ("product", 2, 1),
    ("s2", 1, 0),
    ("s2", 1, 1),
    ("s3", 0, 1),
    ("product", 3, 0),
    ("s1", 2, 1),
    ("final_order", 0, 0),
    ("s1", 2, 0),
    ("s3", 1, 0),
    ("s4", 0, 1),
    ("s3", 1, 1),
    ("s4", 0, 0),
    ("s1", 3, 1),
    ("s1", 3, 0),
    ("query_out", 0, 0),
    ("turns", 0, 0),
    ("s4", 1, 0),
    ("s4", 1, 1),
    ("attention", 0, 0),
    ("s2", 2, 0),
    ("s2", 2, 1),
    ("s2", 3, 1),
    ("hidden", 1, 0),
    ("s2", 3, 0),
    ("g1", 1, 0),
    ("hidden", 1, 1),
    ("attention", 1, 0),
    ("s3", 2, 1),
    ("attended", 0, 0),
    ("g1", 0, 1),
    ("g1", 0, 0),
    ("s3", 2, 0),
    ("s3", 3, 0),
    ("s4", 2, 0),
    ("s3", 3, 1),
    ("g1", 1, 1),
    ("g2", 0, 1),
    ("s4", 2, 1),
    ("s4", 3, 1),
    ("s4", 3, 0),
    ("g2", 0, 0),
    ("g2", 1, 0),
    ("hidden", 2, 0),
    ("g2", 1, 1),
    ("hidden", 2, 1),
    ("g1", 2, 1),
    ("g1", 2, 0),
    ("hidden", 3, 1),
    ("g1", 3, 1),
    ("g3", 0, 1),
    ("g3", 1, 0),
    ("hidden", 3, 0),
    ("g3", 0, 0),
    ("g2", 3, 1),
    ("g1", 3, 0),
    ("g3", 1, 1),
    ("g2", 2, 0),
    ("g2", 3, 0),
    ("g4", 1, 0),
    ("g4", 0, 1),
    ("g2", 2, 1),
    ("g4", 0, 0),
    ("g3", 2, 0),
    ("g3", 3, 1),
    ("second", 0, 1),
    ("g3", 2, 1),
    ("g4", 1, 1),
    ("g3", 3, 0),
    ("g4", 2, 0),
    ("second", 1, 0),
    ("second", 0, 0),
    ("g4", 2, 1),
    ("second", 1, 1),
    ("g4", 3, 0),
    ("g4", 3, 1),
    ("second", 2, 0),
    ("second", 2, 1),
    ("second_early", 3, 1),
    ("second_early", 3, 0),
    ("second_late", 3, 0),
    ("second_late", 3, 1),
)
SENDS, RECVS, LOADS = 39, 79, 19


def dot(a, b):
    return jnp.dot(a, b, preferred_element_type=F32)


def dot_t(a, b):
    return lax.dot_general(a, b, (((1,), (1,)), ((), ())), preferred_element_type=F32)


def iota(shape, dim):
    return lax.broadcasted_iota(jnp.int32, shape, dim)


def one_hot(mask):
    return jnp.where(mask, 1.0, 0.0).astype(BF)


def add_f32(*terms):
    total = terms[0].astype(F32)
    for term in terms[1:]:
        total = total + term.astype(F32)
    return total


class Scratch:
    def __init__(self):
        self.names, self.shapes = [], []

    def add(self, name, shape, dtype=BF):
        self.names.append(name)
        self.shapes.append(pltpu.VMEM(shape, dtype))


def query_width(f):
    return 768 + 128 * f


def scratch_plan(columns):
    s = Scratch()
    for f in range(2):
        for k in range(1 + len(HIDDEN_CHUNKS)):
            hc = 768 if k == 0 else HIDDEN_CHUNKS[k - 1]
            w = query_width(f) if k == 0 else 2 * hc
            t = (k, f)
            s.add(("w1",) + t, (columns, w))
            s.add(("part",) + t, (4, 4, 32, w))
            s.add(("r1",) + t, (2, 2, 32, w))
            s.add(("r2",) + t, (2, 4, 32, w))
            s.add(("q1",) + t, (2, 16, w))
            s.add(("q2",) + t, (2, 32, w))
            s.add(("ag",) + t, (4, 4, 32, hc))
            s.add(("w2",) + t, (hc, columns))
    s.add("keys", (2, 2048, 256))
    s.add("values", (2, 2048, 256))
    s.add("tk", (8, 64, columns))
    s.add("order", (2, 512, 512))
    s.add("xs", (2, 512, columns))
    s.add("acc", (16, 32, columns), F32)
    s.add("ob", (2, 4, 64, columns))
    s.add("fr", (4, 64, columns))
    s.add("fz1", (2, 32, columns))
    s.add("fz2", (2, 64, columns))
    s.add("qsend", (8, 32, 256))
    s.add("qrecv", (8, 32, 256))
    s.add("asend", (8, 32, 256))
    s.add("arecv", (8, 32, 256))
    s.add("inv", (32, 128), F32)
    s.add("turn", (2, 8, 128), F32)
    return s


class Half:
    pass


def kernel(
    plan_names,
    model_width,
    tok,
    gain,
    wq,
    wsh,
    wg,
    wu,
    wo,
    wd,
    kc,
    vc,
    lens,
    frequency,
    out,
    entries,
    *scratch,
):
    n = len(plan_names)
    b = dict(zip(plan_names, scratch[:n]))
    send_sem, recv_sem, local_sem = scratch[n:]
    columns = tok.shape[1]
    g = lax.axis_index("gx")
    q = lax.axis_index("yz")
    z, c = g // 2, lax.rem(g, 2)
    y, x = q // 4, lax.rem(q, 4)

    def step(v, d):
        return lax.rem(v + d + RING, RING)

    def at_x(d):
        return (g, y * 4 + step(x, d))

    def at_y(d):
        return (g, step(y, d) * 4 + x)

    def at_z(d):
        return (step(z, d) * 2 + c, q)

    partner = (z * 2 + 1 - c, q)

    sends, counts = [], {"send": 0, "recv": 0, "load": 0}

    def fresh(kind):
        counts[kind] += 1
        return counts[kind] - 1

    class Flight:
        def __init__(self, arriving):
            self.arriving, self.at = arriving, fresh("recv")

        def wait(self):
            pltpu.make_async_copy(self.arriving, self.arriving, recv_sem.at[self.at]).wait()

    def leaving(ref):
        at = fresh("send")
        sends.append((ref, at))
        return at

    def rc(src, dst, dev, flight, at):
        pltpu.make_async_remote_copy(
            src_ref=src,
            dst_ref=dst,
            send_sem=send_sem.at[at],
            recv_sem=recv_sem.at[flight.at],
            device_id=dev,
            device_id_type=MESH,
        ).start()

    loads = {}

    def load(name, whole, *pairs):
        at = fresh("load")
        for src, dst in pairs:
            pltpu.make_async_copy(src, dst, local_sem.at[at]).start()
        loads[name] = (whole, at)

    def loaded(name):
        whole, at = loads[name]
        pltpu.make_async_copy(whole, whole, local_sem.at[at]).wait()

    load("tok", b["tk"].at[g], (tok, b["tk"].at[g]))
    shared_at = pl.multiple_of(z * 128, 128)
    w1 = b["w1", 0, 1]
    load(
        ("w1", 0, 1),
        w1,
        (wq.at[:, 768:1536], w1.at[:, 0:768]),
        (wsh.at[:, pl.ds(shared_at, 128)], w1.at[:, 768:896]),
    )
    load(("w1", 0, 0), b["w1", 0, 0], (wq.at[:, 0:768], b["w1", 0, 0]))
    hidden_at = {}
    base = 0
    for k, hc in enumerate(HIDDEN_CHUNKS, 1):
        for f in range(2):
            hidden_at[k, f] = base
            base += hc

    def load_w1(k):
        hc = HIDDEN_CHUNKS[k - 1]
        for f in range(2):
            at = hidden_at[k, f]
            w1 = b["w1", k, f]
            load(
                ("w1", k, f),
                w1,
                (wg.at[:, at : at + hc], w1.at[:, 0:hc]),
                (wu.at[:, at : at + hc], w1.at[:, hc : 2 * hc]),
            )

    barrier = pltpu.get_barrier_semaphore()
    others = [lax.rem(g + d, 8) for d in range(1, 8)]
    peers = [at_x(1), at_x(-1), at_y(1), at_y(-1)] + [(o, q) for o in others]
    for peer in peers:
        pl.semaphore_signal(barrier, inc=1, device_id=peer, device_id_type=MESH)
    loaded("tok")
    pl.semaphore_wait(barrier, len(peers))

    tk = b["tk"]

    def block(zz):
        return zz * 2 + c

    zr, zl, zo = step(z, 1), step(z, -1), step(z, 2)
    parts = (pl.ds(0, 32), pl.ds(32, 32))

    token_sends = leaving(tk.at[0:7])
    crossing = Flight(tk.at[0:4])

    def send(blk, i, dev, flight=None):
        ref = tk.at[blk, parts[i]]
        flight = flight or Flight(ref)
        rc(ref, ref, dev, flight, token_sends)
        return flight

    def cross(blk, i):
        send(blk, i, partner, crossing)

    right_first = send(g, 0, at_z(1))
    left_first = send(g, 1, at_z(-1))
    right_last = send(g, 1, at_z(1))
    left_last = send(g, 0, at_z(-1))
    cross(g, 0)
    cross(g, 1)
    for k in range(1, 1 + len(HIDDEN_CHUNKS)):
        load_w1(k)
    row_i, col_i = iota((512, 512), 0), iota((512, 512), 1)
    tail = (((row_i >> 2) & 7) << 6) | (((row_i >> 1) & 1) << 5) | (row_i & 1)
    d1, d2 = (row_i >> 7) & 3, (row_i >> 5) & 3
    source = {0: tail | (d2 << 3) | (d1 << 1), 1: tail | (d1 << 3) | (d2 << 1)}
    order = b["order"]
    order[1] = one_hot(source[1] == col_i)
    right_first.wait()
    forward_r = send(block(zl), 0, at_z(1))
    cross(block(zl), 0)
    left_first.wait()
    forward_l = send(block(zr), 1, at_z(-1))
    cross(block(zr), 1)
    order[0] = one_hot(source[0] == col_i)
    right_last.wait()
    cross(block(zl), 1)
    left_last.wait()
    cross(block(zr), 0)
    forward_r.wait()
    cross(block(zo), 0)
    forward_l.wait()
    cross(block(zo), 1)
    crossing.wait()

    squares = []
    gain_row = gain[...].reshape(1, columns)

    def ordered(f):
        rows = dot(order[f], tk[...].reshape(512, columns))
        if f == 1:
            squares.append(jnp.sum(rows * rows, axis=1, keepdims=True))
        b["xs"][f] = (rows * gain_row).astype(BF)

    def more_loads():
        for k in range(1 + len(HIDDEN_CHUNKS)):
            for f in range(2):
                w2 = b["w2", k, f]
                if k == 0:
                    load(("w2", k, f), w2, (wo.at[768 * f : 768 * f + 768], w2))
                else:
                    at = hidden_at[k, f]
                    load(("w2", k, f), w2, (wd.at[at : at + HIDDEN_CHUNKS[k - 1]], w2))
        load("keys", b["keys"], (kc, b["keys"]))
        load("values", b["values"], (vc, b["values"]))

    lane = iota((1, 128), 1)
    mine = (lane >> 6) == c
    spread = 1.0 + (lane & 63).astype(F32) * (1.0 / 64.0)

    halves = {}
    for f in range(2):
        h = Half()
        first, second = (at_x, at_y) if f == 0 else (at_y, at_x)
        p1, p2 = (x, y) if f == 0 else (y, x)
        h.first, h.second, h.p1, h.p2 = first, second, p1, p2
        h.r1, h.l1, h.o1 = step(p1, 1), step(p1, -1), step(p1, 2)
        h.r2, h.l2, h.o2 = step(p2, 1), step(p2, -1), step(p2, 2)
        halves[f] = h
    cps = {}

    def product(k, f):
        loaded(("w1", k, f))
        part, w1 = b["part", k, f], b["w1", k, f]
        w = 768 if k == 0 else w1.shape[1]

        @pl.loop(0, w // 256)
        def _(i):
            at = pl.ds(pl.multiple_of(i * 256, 256), 256)
            value = dot(b["xs"][f], w1[:, at]).astype(BF)
            part[:, :, :, at] = value.reshape(4, 4, 32, 256)

        if k == 0 and f == 1:
            value = dot(b["xs"][f], w1[:, 768:896])
            value = jnp.where(mine, value, squares[0] * spread).astype(BF)
            part[:, :, :, 768:896] = value.reshape(4, 4, 32, 128)

    def s1(k, f):
        h, part, r1, r2 = halves[f], b["part", k, f], b["r1", k, f], b["r2", k, f]
        one, two, at = Flight(r1), Flight(r2), leaving(part.at[0:3])
        rc(part.at[h.o1, 0:2], r1.at[0], h.first(1), one, at)
        rc(part.at[h.o1, 2:4], r1.at[1], h.first(-1), one, at)
        rc(part.at[h.r1, 2:4], r2.at[0, 2:4], h.first(1), two, at)
        rc(part.at[h.l1, 0:2], r2.at[1, 0:2], h.first(-1), two, at)
        cps[k, f] = one, two, at

    def s2(k, f):
        h, part, r1, r2 = halves[f], b["part", k, f], b["r1", k, f], b["r2", k, f]
        one, two, at = cps[k, f]
        one.wait()
        part[h.r1, 0:2] = add_f32(part[h.r1, 0:2], r1[0]).astype(BF)
        rc(part.at[h.r1, 0:2], r2.at[0, 0:2], h.first(1), two, at)
        part[h.l1, 2:4] = add_f32(part[h.l1, 2:4], r1[1]).astype(BF)
        rc(part.at[h.l1, 2:4], r2.at[1, 2:4], h.first(-1), two, at)

    def s3(k, f):
        h, part, r2 = halves[f], b["part", k, f], b["r2", k, f]
        q1, q2 = b["q1", k, f], b["q2", k, f]
        cps[k, f][1].wait()

        def total(d):
            part[h.p1, d] = add_f32(part[h.p1, d], r2[0, d], r2[1, d]).astype(BF)

        one, two, at = Flight(q1), Flight(q2), leaving(part.at[0, 0:3])
        total(h.o2)
        rc(part.at[h.p1, h.o2, 0:16], q1.at[0], h.second(1), one, at)
        rc(part.at[h.p1, h.o2, 16:32], q1.at[1], h.second(-1), one, at)
        total(h.r2)
        rc(part.at[h.p1, h.r2, 16:32], q2.at[0, 16:32], h.second(1), two, at)
        total(h.l2)
        rc(part.at[h.p1, h.l2, 0:16], q2.at[1, 0:16], h.second(-1), two, at)
        total(h.p2)
        cps[k, f] = one, two, at

    def s4(k, f):
        h, part = halves[f], b["part", k, f]
        q1, q2 = b["q1", k, f], b["q2", k, f]
        one, two, at = cps[k, f]
        one.wait()
        part[h.p1, h.r2, 0:16] = add_f32(part[h.p1, h.r2, 0:16], q1[0]).astype(BF)
        rc(part.at[h.p1, h.r2, 0:16], q2.at[0, 0:16], h.second(1), two, at)
        part[h.p1, h.l2, 16:32] = add_f32(part[h.p1, h.l2, 16:32], q1[1]).astype(BF)
        rc(part.at[h.p1, h.l2, 16:32], q2.at[1, 16:32], h.second(-1), two, at)

    def s5(k, f, lo, hi):
        h, part, q2 = halves[f], b["part", k, f], b["q2", k, f]
        return add_f32(part[h.p1, h.p2, :, lo:hi], q2[0, :, lo:hi], q2[1, :, lo:hi])

    def s5_wait(k, f):
        cps[k, f][1].wait()

    def hidden(k, f):
        s5_wait(k, f)
        h, hc = halves[f], HIDDEN_CHUNKS[k - 1]
        inv = b["inv"][:, 0:1]
        gate = s5(k, f, 0, hc) * inv
        up = s5(k, f, hc, 2 * hc) * inv
        value = gate * (1.0 / (1.0 + jnp.exp(-gate))) * up
        b["ag", k, f][h.p2, h.p1] = value.astype(BF)

    def g1(k, f):
        h, ag = halves[f], b["ag", k, f]
        one, two, at = Flight(ag.at[0, 0:2]), Flight(ag.at[0, 0]), leaving(ag.at[0, 0:3])
        blk = ag.at[h.p2, h.p1]
        rc(blk, blk, h.first(1), one, at)
        rc(blk, blk, h.first(-1), one, at)
        cps["g", k, f] = one, two, at

    def g2(k, f):
        h, ag = halves[f], b["ag", k, f]
        one, two, at = cps["g", k, f]
        one.wait()
        blk = ag.at[h.p2, h.l1, 0:16]
        rc(blk, blk, h.first(1), two, at)
        blk = ag.at[h.p2, h.r1, 16:32]
        rc(blk, blk, h.first(-1), two, at)

    def g3(k, f):
        h, ag = halves[f], b["ag", k, f]
        cps["g", k, f][1].wait()
        one, two, at = Flight(ag.at[0:2]), Flight(ag.at[0]), leaving(ag.at[0:3])
        blk = ag.at[h.p2]
        rc(blk, blk, h.second(1), one, at)
        rc(blk, blk, h.second(-1), one, at)
        cps["g", k, f] = one, two, at

    def g4(k, f):
        h, ag = halves[f], b["ag", k, f]
        one, two, at = cps["g", k, f]
        one.wait()
        blk = ag.at[h.l2, 0:2]
        rc(blk, blk, h.second(1), two, at)
        blk = ag.at[h.r2, 2:4]
        rc(blk, blk, h.second(-1), two, at)

    first_product = [True]

    def second(k, f):
        cps["g", k, f][1].wait()
        loaded(("w2", k, f))
        ag, w2, acc = b["ag", k, f], b["w2", k, f], b["acc"]
        start = first_product[0]
        first_product[0] = False
        for lo, hi in ((0, 256), (256, 512), (512, columns)):
            value = dot(ag[...].reshape(512, ag.shape[3]), w2[:, lo:hi])
            value = value.reshape(16, 32, hi - lo)
            for i in range(16):
                to = i if f == 0 else i % 4 * 4 + i // 4
                if start:
                    acc[to, :, lo:hi] = value[i]
                else:
                    acc[to, :, lo:hi] += value[i]

    def second_rows(k, f, d):
        ag, w2, acc = b["ag", k, f], b["w2", k, f], b["acc"]
        value = dot(ag[d].reshape(128, ag.shape[3]), w2[...]).reshape(4, 32, columns)
        for i in range(4):
            at = d * 4 + i if f == 0 else i * 4 + d
            acc[at] += value[i]

    def second_early(k, f):
        h = halves[f]
        loaded(("w2", k, f))
        for d in (h.p2, h.l2, h.r2):
            second_rows(k, f, d)

    def second_late(k, f):
        cps["g", k, f][1].wait()
        second_rows(k, f, halves[f].o2)

    def exchange(send, recv):
        flight, at = Flight(recv.at[0:7]), leaving(send.at[0:7])
        for o in others:
            rc(send.at[o], recv.at[g], (o, q), flight, at)
        recv[g] = send[g]
        return flight

    def spread_rows(head):
        row, col = iota((256, 32), 0), iota((256, 32), 1)
        return one_hot((col == (((row >> 5) << 2) | (row & 3))) & (((row >> 2) & 7) == head))

    def collect_rows(head):
        row, col = iota((32, 256), 0), iota((32, 256), 1)
        return one_hot((row == (((col >> 5) << 2) | (col & 3))) & (((col >> 2) & 7) == head))

    def query_out():
        s5_wait(0, 0)
        s5_wait(0, 1)
        shared = s5(0, 1, 768, 896)
        total = jnp.sum(jnp.where(mine, 0.0, shared), axis=1, keepdims=True) * (1.0 / 95.5)
        inv = lax.rsqrt(total / model_width + EPSILON)
        b["inv"][...] = jnp.broadcast_to(inv, (32, 128))
        shared = jnp.where(mine, shared * inv, 0.0)
        low = lax.rem(z, 2) == 0
        shared = jnp.concatenate([jnp.where(low, shared, 0.0), jnp.where(low, 0.0, shared)], axis=1)
        rows = dot(spread_rows(6), shared.astype(BF))
        for f in range(2):
            for i in range(3):
                piece = (s5(0, f, i * 256, i * 256 + 256) * inv).astype(BF)
                rows = rows + dot(spread_rows(f * 3 + i), piece)
        b["qsend"][...] = rows.astype(BF).reshape(8, 32, 256)
        cps["q"] = exchange(b["qsend"], b["qrecv"])

    def rotate(rows):
        count = rows.shape[0]
        rows = rows.reshape(count // 8, 8, 256)
        front, back = rows[:, :, :128], rows[:, :, 128:]
        cosine, sine = b["turn"][0][None], b["turn"][1][None]
        return jnp.concatenate(
            [front * cosine - back * sine, back * cosine + front * sine], axis=2
        ).reshape(count, 256)

    def turns():
        row = iota((8, 128), 0)
        position = jnp.where((row & 1) == 0, lens[0], lens[1]) + ((row >> 1) & 1)
        angles = position.astype(F32) * frequency[...]
        b["turn"][0] = jnp.cos(angles)
        b["turn"][1] = jnp.sin(angles)

    def attention():
        cps["q"].wait()
        loaded("keys")
        loaded("values")
        raw = b["qrecv"][...].reshape(256, 256)
        queries = rotate(raw.astype(F32)).astype(BF)
        row, col = iota((128, 256), 0), iota((128, 256), 1)
        pick = (row < 4) & ((col & 31) == row + 24)
        key_now = rotate(dot(one_hot(pick & (col < 128)), raw)).astype(BF)
        value_now = dot(one_hot(pick & (col >= 128)), raw).astype(BF)
        for i, part in enumerate((key_now, value_now)):
            fresh_rows = part[0:16].astype(F32)
            for t in range(2):
                entries[t, :, i * 256 : i * 256 + 256] = fresh_rows[2 * t : 2 * t + 2].astype(BF)
        cps["rows"] = queries, key_now, value_now
        attention_row(0)

    def attention_row(j):
        queries, key_now, value_now = cps["rows"]
        row, col = iota((128, 256), 0), iota((128, 256), 1)
        chosen = one_hot(col == (((row >> 4) << 5) + ((row & 15) << 1) + j))
        heads = dot(chosen, queries).astype(BF)
        scores = dot_t(heads, b["keys"][j]) * (1.0 / 16.0)
        live = iota(scores.shape, 1) < lens[j]
        scores = jnp.where(live, scores, -jnp.inf)
        now = dot_t(heads, key_now) * (1.0 / 16.0)
        r, n_ = iota((128, 128), 0), iota((128, 128), 1)
        now = jnp.where((n_ < 4) & ((n_ & 1) == j) & ((n_ >> 1) <= (r & 1)), now, -jnp.inf)
        top = jnp.maximum(
            jnp.max(scores, axis=1, keepdims=True), jnp.max(now, axis=1, keepdims=True)
        )
        scores = jnp.exp(scores - top)
        now = jnp.exp(now - top)
        under = jnp.sum(scores, axis=1, keepdims=True) + jnp.sum(now, axis=1, keepdims=True)
        scale = 1.0 / under
        mixed = dot((scores * scale).astype(BF), b["values"][j]) + dot(
            (now * scale).astype(BF), value_now
        )
        brow, bcol = iota((256, 128), 0), iota((256, 128), 1)
        back = one_hot(brow == (((bcol >> 4) << 5) + ((bcol & 15) << 1) + j))
        term = dot(back, mixed.astype(BF))
        if j == 0:
            cps["term"] = term
            return
        result = cps["term"] + term
        b["asend"][...] = result.astype(BF).reshape(8, 32, 256)
        cps["a"] = exchange(b["asend"], b["arecv"])

    def attended():
        cps["a"].wait()
        raw = b["arecv"][...].reshape(256, 256)
        for f in range(2):
            h = halves[f]
            for i in range(3):
                value = dot(collect_rows(f * 3 + i), raw).astype(BF)
                b["ag", 0, f][h.p2, h.p1, :, i * 256 : i * 256 + 256] = value

    def final_order():
        gx_o = (((row_i >> 6) & 3) << 1) | (row_i >> 8)
        wanted = (((row_i >> 1) & 15) << 5) | (gx_o << 2) | (((row_i >> 5) & 1) << 1) | (row_i & 1)
        order[0] = one_hot(wanted == col_i)

    stages = {
        "ordered": lambda k, f: ordered(f),
        "query_out": lambda k, f: query_out(),
        "attention": lambda k, f: attention_row(1) if k else attention(),
        "attended": lambda k, f: attended(),
        "turns": lambda k, f: turns(),
        "final_order": lambda k, f: final_order(),
        "more_loads": lambda k, f: more_loads(),
    }
    for stage in (product, s1, s2, s3, s4, hidden, g1, g2, g3, g4, second, second_early, second_late):
        stages[stage.__name__] = stage

    ordered(1)
    for name, k, f in ORDER:
        stages[name](k, f)

    ob, fr, fz1, fz2 = b["ob"], b["fr"], b["fz1"], b["fz2"]
    spans = (slice(0, 384), slice(384, columns))
    top, low = slice(0, 32), slice(32, 64)
    crossed = []
    for span in spans:
        rows = b["acc"][:, :, span].reshape(512, -1).astype(BF)
        ob[:, :, :, span] = dot(order[0], rows).astype(BF).reshape(2, 4, 64, -1)
        flight = Flight(fr.at[:, :, span])
        rc(ob.at[1 - c, :, :, span], fr.at[:, :, span], partner, flight, leaving(fr.at[:, :, span]))
        crossed.append(flight)
    waves = []
    for i, span in enumerate(spans):
        crossed[i].wait()

        def add_partner(zz):
            ob[c, zz, :, span] = add_f32(ob[c, zz, :, span], fr[zz, :, span]).astype(BF)

        one, two = Flight(fz1.at[:, :, span]), Flight(fz2.at[:, :, span])
        at = leaving(fr.at[0:3, :, span])
        add_partner(zo)
        rc(ob.at[c, zo, top, span], fz1.at[0, :, span], at_z(1), one, at)
        rc(ob.at[c, zo, low, span], fz1.at[1, :, span], at_z(-1), one, at)
        add_partner(zr)
        rc(ob.at[c, zr, low, span], fz2.at[0, low, span], at_z(1), two, at)
        add_partner(zl)
        rc(ob.at[c, zl, top, span], fz2.at[1, top, span], at_z(-1), two, at)
        waves.append((one, two, at))
    for i, span in enumerate(spans):
        one, two, at = waves[i]
        one.wait()
        ob[c, zr, top, span] = add_f32(ob[c, zr, top, span], fz1[0, :, span]).astype(BF)
        rc(ob.at[c, zr, top, span], fz2.at[0, top, span], at_z(1), two, at)
        ob[c, zl, low, span] = add_f32(ob[c, zl, low, span], fz1[1, :, span]).astype(BF)
        rc(ob.at[c, zl, low, span], fz2.at[1, low, span], at_z(-1), two, at)
    for i, span in enumerate(spans):
        own = add_f32(ob[c, z, :, span], fr[z, :, span])
        waves[i][1].wait()
        own = own + fz2[0, :, span].astype(F32) + fz2[1, :, span].astype(F32)
        out[:, :, span] = own.reshape(2, 32, -1)
    for ref, at in sends:
        pltpu.make_async_copy(ref, ref, send_sem.at[at]).wait()
    assert counts == {"send": SENDS, "recv": RECVS, "load": LOADS}, counts


def local(
    tokens,
    norm_gain,
    w_query,
    w_shared,
    w_gate,
    w_up,
    w_out,
    w_down,
    key_cache,
    value_cache,
    lengths,
):
    steps, block_rows, columns = tokens.shape
    model_width = columns * lax.axis_size("yz")
    frequency = np.exp(np.arange(128, dtype=np.float32) * np.float32(-2.0 * math.log(10000.0) / 256))
    plan = scratch_plan(columns)
    hbm = pl.BlockSpec(memory_space=pl.ANY)
    vmem = pl.BlockSpec(memory_space=pltpu.VMEM)
    smem = pl.BlockSpec(memory_space=pltpu.SMEM)
    layer, entries = pl.pallas_call(
        functools.partial(kernel, plan.names, model_width),
        out_shape=(
            jax.ShapeDtypeStruct((steps, block_rows, columns), F32),
            jax.ShapeDtypeStruct((2, 2, 512), BF),
        ),
        in_specs=[hbm, vmem] + [hbm] * 8 + [smem, vmem],
        out_specs=(vmem, vmem),
        scratch_shapes=plan.shapes
        + [
            pltpu.SemaphoreType.DMA((SENDS,)),
            pltpu.SemaphoreType.DMA((RECVS,)),
            pltpu.SemaphoreType.DMA((LOADS,)),
        ],
        compiler_params=pltpu.CompilerParams(
            collective_id=0, has_side_effects=True, vmem_limit_bytes=64 << 20
        ),
        cost_estimate=pl.CostEstimate(
            flops=12 * 10**9, bytes_accessed=28 * 10**6, transcendentals=10**6
        ),
    )(
        tokens.reshape(steps * block_rows, columns),
        norm_gain,
        w_query,
        w_shared,
        w_gate,
        w_up,
        w_out,
        w_down,
        key_cache,
        value_cache,
        lengths,
        jnp.asarray(frequency[None]),
    )
    return (tokens.astype(F32) + layer).astype(BF), entries


def solution(mesh):
    in_specs = (
        P(None, "gx", "yz"),
        P("yz"),
        P("yz", "gx"),
        P("yz", None),
        P("yz", "gx"),
        P("yz", "gx"),
        P("gx", "yz"),
        P("gx", "yz"),
        P(("gx", "yz"), None, None),
        P(("gx", "yz"), None, None),
        P(("gx", "yz")),
    )
    out_specs = (P(None, "gx", "yz"), P(None, ("gx", "yz"), None))
    return jax.shard_map(local, mesh=mesh, in_specs=in_specs, out_specs=out_specs, check_vma=False)
```

time: 138 us -> 130 us (0.942)
  Pallas kernels: 131 us -> 126 us
  local copies, waits for them, and re-layouts: 5.41 us -> 1.28 us
    pallas_call x1, Pallas kernels: 131 us -> 126 us  [local(): pl.pallas_call(functools.partial(kernel, plan.names, model_width), out_sh...]
    convert_element_type x1, other arithmetic: 0.01 us -> 1.62 us  [local(): return ((tokens.astype(F32) + layer).astype(BF), entries)]
where the time goes in v2:
time: 130 us
  Pallas kernels  126 us (97%)
  other arithmetic  1.62 us (1%)
    pallas_call x1, Pallas kernels, local(): pl.pallas_call(functools.partial(kernel, plan.names, model_width), out_sh...  126 us

profile of v2, /device:TPU:1, one launch (start us, length us, event | category | flops | bytes accessed | tf_op | source)
XLA Modules:
  0.0 129.8 jit_solution(10836204273668984418)
XLA Ops:
  0.6 126.3 %shard_map.131 = (f32[2,32,640]{2,1,0:T(8,128)}, bf16[2,2,512]{2,1,0:T(2,128)(2,1)}) custom-call(bf16[64,640]{1,0:T(8,128)(2,1)} %bitcast.1, f32[640]{0:T(1024)} %gain.1, bf16[640,1536]{1,0:T(8,128)(2,1)} %wq.1, bf16[640,512]{1,0:T(8,128)(2,1)} %wsh.1, bf16[640,4608]{1,0:T(8,128)(2,1)} %wg.1, bf16[640,4608]{1,0:T(8,128)(2,1)} %wu.1, bf16[1536,640]{1,0:T(8,128)(2,1)} %wo.1, ...), custom_call_target="tpu_custom_call" | custom-call | flops 12000000000 | bytes 28000000 | tf_op jit(solution)/shard_map/pallas_call | solution.py:739
  126.9 1.6 %add_convert_fusion = bf16[2,32,640]{2,1,0:T(8,128)(2,1)} fusion(f32[2,32,640]{2,1,0:T(8,128)} %get-tuple-element.4, bf16[2,32,640]{2,1,0:T(8,128)(2,1)} %param.12), kind=kLoop, calls=%fused_computation | loop fusion | flops 122880 | bytes 327680 | tf_op jit(solution)/shard_map/convert_element_type | solution.py:773
  128.5 1.3 copy.15

commit v3 on v2

--- a/solution.py
+++ b/solution.py
@@ -16,11 +16,6 @@
 HIDDEN_CHUNKS = (768, 768, 768)
 RING = 4
 ORDER = (
-    ("product", 0, 1),
-    ("s1", 0, 1),
-    ("ordered", 0, 0),
-    ("product", 0, 0),
-    ("s1", 0, 0),
     ("more_loads", 0, 0),
     ("product", 1, 1),
     ("s2", 0, 1),
@@ -113,7 +108,7 @@
     ("second_late", 3, 0),
     ("second_late", 3, 1),
 )
-SENDS, RECVS, LOADS = 39, 79, 19
+SENDS, RECVS, LOADS = 39, 80, 19
 
 
 def dot(a, b):
@@ -171,7 +166,7 @@
     s.add("values", (2, 2048, 256))
     s.add("tk", (8, 64, columns))
     s.add("order", (2, 512, 512))
-    s.add("xs", (2, 512, columns))
+    s.add("xs", (2, 2, 256, columns))
     s.add("acc", (16, 32, columns), F32)
     s.add("ob", (2, 4, 64, columns))
     s.add("fr", (4, 64, columns))
@@ -272,6 +267,12 @@
         whole, at = loads[name]
         pltpu.make_async_copy(whole, whole, local_sem.at[at]).wait()
 
+    barrier = pltpu.get_barrier_semaphore()
+    others = [lax.rem(g + d, 8) for d in range(1, 8)]
+    peers = [at_x(1), at_x(-1), at_y(1), at_y(-1)] + [(o, q) for o in others]
+    for peer in peers:
+        pl.semaphore_signal(barrier, inc=1, device_id=peer, device_id_type=MESH)
+
     load("tok", b["tk"].at[g], (tok, b["tk"].at[g]))
     shared_at = pl.multiple_of(z * 128, 128)
     w1 = b["w1", 0, 1]
@@ -301,11 +302,6 @@
                 (wu.at[:, at : at + hc], w1.at[:, hc : 2 * hc]),
             )
 
-    barrier = pltpu.get_barrier_semaphore()
-    others = [lax.rem(g + d, 8) for d in range(1, 8)]
-    peers = [at_x(1), at_x(-1), at_y(1), at_y(-1)] + [(o, q) for o in others]
-    for peer in peers:
-        pl.semaphore_signal(barrier, inc=1, device_id=peer, device_id_type=MESH)
     loaded("tok")
     pl.semaphore_wait(barrier, len(peers))
 
@@ -318,7 +314,7 @@
     parts = (pl.ds(0, 32), pl.ds(32, 32))
 
     token_sends = leaving(tk.at[0:7])
-    crossing = Flight(tk.at[0:4])
+    near, far = Flight(tk.at[0:2]), Flight(tk.at[0:2])
 
     def send(blk, i, dev, flight=None):
         ref = tk.at[blk, parts[i]]
@@ -326,48 +322,47 @@
         rc(ref, ref, dev, flight, token_sends)
         return flight
 
-    def cross(blk, i):
-        send(blk, i, partner, crossing)
-
+    def cross(blk, i, flight):
+        send(blk, i, partner, flight)
+
+    left_first = send(g, 1, at_z(-1))
     right_first = send(g, 0, at_z(1))
-    left_first = send(g, 1, at_z(-1))
+    left_last = send(g, 0, at_z(-1))
     right_last = send(g, 1, at_z(1))
-    left_last = send(g, 0, at_z(-1))
-    cross(g, 0)
-    cross(g, 1)
+    cross(g, 0, near)
+    cross(g, 1, near)
     for k in range(1, 1 + len(HIDDEN_CHUNKS)):
         load_w1(k)
-    row_i, col_i = iota((512, 512), 0), iota((512, 512), 1)
-    tail = (((row_i >> 2) & 7) << 6) | (((row_i >> 1) & 1) << 5) | (row_i & 1)
-    d1, d2 = (row_i >> 7) & 3, (row_i >> 5) & 3
-    source = {0: tail | (d2 << 3) | (d1 << 1), 1: tail | (d1 << 3) | (d2 << 1)}
+    row_i, col_i = iota((256, 256), 0), iota((256, 256), 1)
+    tail = (((row_i >> 2) & 3) << 6) | (((row_i >> 1) & 1) << 5) | (row_i & 1)
+    d1, d2 = (row_i >> 6) & 3, (row_i >> 4) & 3
     order = b["order"]
-    order[1] = one_hot(source[1] == col_i)
+    order[0, 0:256, 0:256] = one_hot((tail | (d2 << 3) | (d1 << 1)) == col_i)
+    order[1, 0:256, 0:256] = one_hot((tail | (d1 << 3) | (d2 << 1)) == col_i)
+    left_first.wait()
+    forward_l = send(block(zr), 1, at_z(-1))
+    cross(block(zr), 1, near)
     right_first.wait()
     forward_r = send(block(zl), 0, at_z(1))
-    cross(block(zl), 0)
-    left_first.wait()
-    forward_l = send(block(zr), 1, at_z(-1))
-    cross(block(zr), 1)
-    order[0] = one_hot(source[0] == col_i)
+    left_last.wait()
+    cross(block(zr), 0, near)
+    cross(block(zl), 0, far)
     right_last.wait()
-    cross(block(zl), 1)
-    left_last.wait()
-    cross(block(zr), 0)
-    forward_r.wait()
-    cross(block(zo), 0)
-    forward_l.wait()
-    cross(block(zo), 1)
-    crossing.wait()
-
-    squares = []
+    cross(block(zl), 1, far)
+    near.wait()
+
+    squares = {}
     gain_row = gain[...].reshape(1, columns)
 
-    def ordered(f):
-        rows = dot(order[f], tk[...].reshape(512, columns))
+    def position(gx):
+        return ((((gx >> 1) + 4 - z) & 3) << 1) | (gx & 1)
+
+    def ordered(f, group):
+        planes = [tk[pl.ds(step(z, 2 * group + i) * 2, 2)].reshape(128, columns) for i in range(2)]
+        rows = dot(order[f, 0:256, 0:256], jnp.concatenate(planes, axis=0))
         if f == 1:
-            squares.append(jnp.sum(rows * rows, axis=1, keepdims=True))
-        b["xs"][f] = (rows * gain_row).astype(BF)
+            squares[group] = jnp.sum(rows * rows, axis=1, keepdims=True)
+        b["xs"][f, group] = (rows * gain_row).astype(BF)
 
     def more_loads():
         for k in range(1 + len(HIDDEN_CHUNKS)):
@@ -398,19 +393,40 @@
 
     def product(k, f):
         loaded(("w1", k, f))
-        part, w1 = b["part", k, f], b["w1", k, f]
-        w = 768 if k == 0 else w1.shape[1]
-
-        @pl.loop(0, w // 256)
+        part, w1, xs = b["part", k, f], b["w1", k, f], b["xs"]
+
+        @pl.loop(0, w1.shape[1] // 256)
         def _(i):
             at = pl.ds(pl.multiple_of(i * 256, 256), 256)
-            value = dot(b["xs"][f], w1[:, at]).astype(BF)
-            part[:, :, :, at] = value.reshape(4, 4, 32, 256)
-
-        if k == 0 and f == 1:
-            value = dot(b["xs"][f], w1[:, 768:896])
-            value = jnp.where(mine, value, squares[0] * spread).astype(BF)
-            part[:, :, :, 768:896] = value.reshape(4, 4, 32, 128)
+            value = dot(xs[f].reshape(512, columns), w1[:, at]).astype(BF)
+            value = value.reshape(2, 4, 4, 16, 256)
+            part[:, :, 0:16, at] = value[0]
+            part[:, :, 16:32, at] = value[1]
+
+    def product_group(f, group):
+        if group == 0:
+            loaded(("w1", 0, f))
+        part, w1, xs = b["part", 0, f], b["w1", 0, f], b["xs"]
+        lines = slice(16 * group, 16 * group + 16)
+        for i in range(3):
+            at = slice(i * 256, i * 256 + 256)
+            value = dot(xs[f, group], w1[:, at]).astype(BF)
+            part[:, :, lines, at] = value.reshape(4, 4, 16, 256)
+        if f == 1:
+            value = dot(xs[f, group], w1[:, 768:896])
+            value = jnp.where(mine, value, squares[group] * spread).astype(BF)
+            part[:, :, lines, 768:896] = value.reshape(4, 4, 16, 128)
+
+    def s1_group(f, group):
+        h, part, r1, r2 = halves[f], b["part", 0, f], b["r1", 0, f], b["r2", 0, f]
+        if group == 0:
+            cps[0, f] = Flight(r1), Flight(r2), leaving(part.at[0:3])
+        one, two, at = cps[0, f]
+        lines = slice(16 * group, 16 * group + 16)
+        rc(part.at[h.o1, 0:2, lines], r1.at[0, :, lines], h.first(1), one, at)
+        rc(part.at[h.o1, 2:4, lines], r1.at[1, :, lines], h.first(-1), one, at)
+        rc(part.at[h.r1, 2:4, lines], r2.at[0, 2:4, lines], h.first(1), two, at)
+        rc(part.at[h.l1, 0:2, lines], r2.at[1, 0:2, lines], h.first(-1), two, at)
 
     def s1(k, f):
         h, part, r1, r2 = halves[f], b["part", k, f], b["r1", k, f], b["r2", k, f]
@@ -554,11 +570,11 @@
 
     def spread_rows(head):
         row, col = iota((256, 32), 0), iota((256, 32), 1)
-        return one_hot((col == (((row >> 5) << 2) | (row & 3))) & (((row >> 2) & 7) == head))
+        return one_hot((col == ((position(row >> 5) << 2) | (row & 3))) & (((row >> 2) & 7) == head))
 
     def collect_rows(head):
         row, col = iota((32, 256), 0), iota((32, 256), 1)
-        return one_hot((row == (((col >> 5) << 2) | (col & 3))) & (((col >> 2) & 7) == head))
+        return one_hot((row == ((position(col >> 5) << 2) | (col & 3))) & (((col >> 2) & 7) == head))
 
     def query_out():
         s5_wait(0, 0)
@@ -652,12 +668,12 @@
                 b["ag", 0, f][h.p2, h.p1, :, i * 256 : i * 256 + 256] = value
 
     def final_order():
-        gx_o = (((row_i >> 6) & 3) << 1) | (row_i >> 8)
-        wanted = (((row_i >> 1) & 15) << 5) | (gx_o << 2) | (((row_i >> 5) & 1) << 1) | (row_i & 1)
-        order[0] = one_hot(wanted == col_i)
+        row, col = iota((512, 512), 0), iota((512, 512), 1)
+        gx = (((row >> 6) & 3) << 1) | (row >> 8)
+        wanted = ((row >> 1) & 15) << 5 | (position(gx) << 2) | (((row >> 5) & 1) << 1) | (row & 1)
+        order[0] = one_hot(wanted == col)
 
     stages = {
-        "ordered": lambda k, f: ordered(f),
         "query_out": lambda k, f: query_out(),
         "attention": lambda k, f: attention_row(1) if k else attention(),
         "attended": lambda k, f: attended(),
@@ -668,7 +684,21 @@
     for stage in (product, s1, s2, s3, s4, hidden, g1, g2, g3, g4, second, second_early, second_late):
         stages[stage.__name__] = stage
 
-    ordered(1)
+    ordered(1, 0)
+    product_group(1, 0)
+    s1_group(1, 0)
+    forward_l.wait()
+    cross(block(zo), 1, far)
+    forward_r.wait()
+    cross(block(zo), 0, far)
+    ordered(0, 0)
+    product_group(0, 0)
+    s1_group(0, 0)
+    far.wait()
+    for f in (1, 0):
+        ordered(f, 1)
+        product_group(f, 1)
+        s1_group(f, 1)
     for name, k, f in ORDER:
         stages[name](k, f)
 

time: 130 us -> 127 us (0.977)
  Pallas kernels: 126 us -> 123 us
    pallas_call x1, Pallas kernels: 126 us -> 123 us  [local(): pl.pallas_call(functools.partial(kernel, plan.names, model_width), out_sh...]
where the time goes in v3:
time: 127 us
  Pallas kernels  123 us (97%)
  other arithmetic  1.62 us (1%)
  local copies, waits for them, and re-layouts  1.28 us (1%)
    pallas_call x1, Pallas kernels, local(): pl.pallas_call(functools.partial(kernel, plan.names, model_width), out_sh...  123 us

profile of v3, /device:TPU:1, one launch (start us, length us, event | category | flops | bytes accessed | tf_op | source)
XLA Modules:
  0.0 126.7 jit_solution(10443542301741959342)
XLA Ops:
  0.6 123.2 %shard_map.131 = (f32[2,32,640]{2,1,0:T(8,128)}, bf16[2,2,512]{2,1,0:T(2,128)(2,1)}) custom-call(bf16[64,640]{1,0:T(8,128)(2,1)} %bitcast.1, f32[640]{0:T(1024)} %gain.1, bf16[640,1536]{1,0:T(8,128)(2,1)} %wq.1, bf16[640,512]{1,0:T(8,128)(2,1)} %wsh.1, bf16[640,4608]{1,0:T(8,128)(2,1)} %wg.1, bf16[640,4608]{1,0:T(8,128)(2,1)} %wu.1, bf16[1536,640]{1,0:T(8,128)(2,1)} %wo.1, ...), custom_call_target="tpu_custom_call" | custom-call | flops 12000000000 | bytes 28000000 | tf_op jit(solution)/shard_map/pallas_call | solution.py:769
  123.8 1.6 %add_convert_fusion = bf16[2,32,640]{2,1,0:T(8,128)(2,1)} fusion(f32[2,32,640]{2,1,0:T(8,128)} %get-tuple-element.4, bf16[2,32,640]{2,1,0:T(8,128)(2,1)} %param.12), kind=kLoop, calls=%fused_computation | loop fusion | flops 122880 | bytes 327680 | tf_op jit(solution)/shard_map/convert_element_type | solution.py:803
  125.4 1.3 %copy.15 = bf16[2,2,512]{2,1,0:T(2,128)(2,1)} copy(bf16[2,2,512]{2,1,0:T(2,128)(2,1)} %get-tuple-element.9) | data formatting | bytes 8192

commit v4 on v3

--- a/solution.py
+++ b/solution.py
@@ -17,94 +17,94 @@
 RING = 4
 ORDER = (
     ("more_loads", 0, 0),
+    ("product", 1, 0),
+    ("s2", 0, 1),
+    ("s1", 1, 0),
     ("product", 1, 1),
-    ("s2", 0, 1),
     ("s1", 1, 1),
+    ("s3", 0, 1),
+    ("product", 2, 1),
+    ("product", 3, 1),
+    ("s2", 1, 1),
     ("s2", 0, 0),
-    ("product", 1, 0),
-    ("s1", 1, 0),
-    ("product", 3, 1),
+    ("s2", 1, 0),
+    ("final_order", 0, 0),
+    ("product", 3, 0),
     ("s3", 0, 0),
+    ("s1", 3, 0),
+    ("s1", 2, 1),
+    ("s4", 0, 1),
+    ("s4", 0, 0),
+    ("turns", 0, 0),
     ("product", 2, 0),
-    ("product", 2, 1),
-    ("s2", 1, 0),
-    ("s2", 1, 1),
-    ("s3", 0, 1),
-    ("product", 3, 0),
-    ("s1", 2, 1),
-    ("final_order", 0, 0),
     ("s1", 2, 0),
+    ("s1", 3, 1),
+    ("s3", 1, 1),
+    ("query_out", 0, 0),
+    ("s2", 2, 1),
+    ("s2", 2, 0),
+    ("attention", 0, 0),
+    ("s2", 3, 0),
     ("s3", 1, 0),
-    ("s4", 0, 1),
-    ("s3", 1, 1),
-    ("s4", 0, 0),
-    ("s1", 3, 1),
-    ("s1", 3, 0),
-    ("query_out", 0, 0),
-    ("turns", 0, 0),
+    ("s2", 3, 1),
+    ("attention", 1, 0),
     ("s4", 1, 0),
+    ("s3", 2, 0),
+    ("s3", 2, 1),
     ("s4", 1, 1),
-    ("attention", 0, 0),
-    ("s2", 2, 0),
-    ("s2", 2, 1),
-    ("s2", 3, 1),
+    ("s3", 3, 0),
     ("hidden", 1, 0),
-    ("s2", 3, 0),
-    ("g1", 1, 0),
-    ("hidden", 1, 1),
-    ("attention", 1, 0),
-    ("s3", 2, 1),
+    ("s4", 2, 1),
     ("attended", 0, 0),
     ("g1", 0, 1),
     ("g1", 0, 0),
-    ("s3", 2, 0),
-    ("s3", 3, 0),
+    ("g1", 1, 0),
+    ("s3", 3, 1),
+    ("hidden", 1, 1),
     ("s4", 2, 0),
-    ("s3", 3, 1),
     ("g1", 1, 1),
     ("g2", 0, 1),
-    ("s4", 2, 1),
-    ("s4", 3, 1),
     ("s4", 3, 0),
     ("g2", 0, 0),
+    ("hidden", 2, 1),
+    ("s4", 3, 1),
+    ("g1", 2, 1),
+    ("g2", 1, 1),
+    ("hidden", 2, 0),
+    ("g1", 2, 0),
+    ("g3", 0, 0),
     ("g2", 1, 0),
-    ("hidden", 2, 0),
-    ("g2", 1, 1),
-    ("hidden", 2, 1),
-    ("g1", 2, 1),
-    ("g1", 2, 0),
+    ("hidden", 3, 0),
     ("hidden", 3, 1),
     ("g1", 3, 1),
     ("g3", 0, 1),
+    ("g3", 1, 1),
     ("g3", 1, 0),
-    ("hidden", 3, 0),
-    ("g3", 0, 0),
+    ("g1", 3, 0),
     ("g2", 3, 1),
-    ("g1", 3, 0),
-    ("g3", 1, 1),
     ("g2", 2, 0),
-    ("g2", 3, 0),
-    ("g4", 1, 0),
-    ("g4", 0, 1),
     ("g2", 2, 1),
     ("g4", 0, 0),
+    ("g4", 0, 1),
+    ("g2", 3, 0),
     ("g3", 2, 0),
-    ("g3", 3, 1),
-    ("second", 0, 1),
     ("g3", 2, 1),
+    ("second", 0, 0),
+    ("g4", 1, 0),
     ("g4", 1, 1),
     ("g3", 3, 0),
     ("g4", 2, 0),
+    ("g3", 3, 1),
     ("second", 1, 0),
-    ("second", 0, 0),
     ("g4", 2, 1),
     ("second", 1, 1),
+    ("g4", 3, 1),
     ("g4", 3, 0),
-    ("g4", 3, 1),
+    ("second", 0, 1),
     ("second", 2, 0),
     ("second", 2, 1),
+    ("second_early", 3, 0),
     ("second_early", 3, 1),
-    ("second_early", 3, 0),
     ("second_late", 3, 0),
     ("second_late", 3, 1),
 )

time: 127 us -> 126 us (level)
    pallas_call x1, Pallas kernels: 123 us -> 122 us  [local(): pl.pallas_call(functools.partial(kernel, plan.names, model_width), out_sh...]
where the time goes in v4:
time: 126 us; the launch traced here: 125 us
  Pallas kernels  122 us (97%)
  other arithmetic  1.62 us (1%)
  local copies, waits for them, and re-layouts  1.28 us (1%)
    pallas_call x1, Pallas kernels, local(): pl.pallas_call(functools.partial(kernel, plan.names, model_width), out_sh...  122 us

profile of v4, /device:TPU:1, one launch (start us, length us, event | category | flops | bytes accessed | tf_op | source)
XLA Modules:
  0.0 125.4 jit_solution(10697858439206648882)
XLA Ops:
  0.6 121.8 %shard_map.131 = (f32[2,32,640]{2,1,0:T(8,128)}, bf16[2,2,512]{2,1,0:T(2,128)(2,1)}) custom-call(bf16[64,640]{1,0:T(8,128)(2,1)} %bitcast.1, f32[640]{0:T(1024)} %gain.1, bf16[640,1536]{1,0:T(8,128)(2,1)} %wq.1, bf16[640,512]{1,0:T(8,128)(2,1)} %wsh.1, bf16[640,4608]{1,0:T(8,128)(2,1)} %wg.1, bf16[640,4608]{1,0:T(8,128)(2,1)} %wu.1, bf16[1536,640]{1,0:T(8,128)(2,1)} %wo.1, ...), custom_call_target="tpu_custom_call" | custom-call | flops 12000000000 | bytes 28000000 | tf_op jit(solution)/shard_map/pallas_call | solution.py:769
  122.5 1.6 %add_convert_fusion = bf16[2,32,640]{2,1,0:T(8,128)(2,1)} fusion(f32[2,32,640]{2,1,0:T(8,128)} %get-tuple-element.4, bf16[2,32,640]{2,1,0:T(8,128)(2,1)} %param.12), kind=kLoop, calls=%fused_computation | loop fusion | flops 122880 | bytes 327680 | tf_op jit(solution)/shard_map/convert_element_type | solution.py:803
  124.1 1.3 %copy.15 = bf16[2,2,512]{2,1,0:T(2,128)(2,1)} copy(bf16[2,2,512]{2,1,0:T(2,128)(2,1)} %get-tuple-element.9) | data formatting | bytes 8192
